TPU v7x, 32 devices: a whole 2x2x4 slice. The times are simulated.
32 devices in a mesh: seg: 16 (over z, y, core), blk: 2 (over x).
Axes of the slice: x: 2, y: 2, z: 4, core: 2. Of those that a mesh axis runs over, the one named last changes fastest.
Arguments:
- state: bfloat16 [16, 4, 128, 2048], P('seg', 'blk'), may hold values from -6 to 6
- left_env: bfloat16 [16, 14, 4, 128, 128], P('seg', None, 'blk'), may hold values from -5 to 5
- right_env: bfloat16 [16, 14, 4, 128, 128], P('seg', None, 'blk'), may hold values from -3 to 3
- site_ops: bfloat16 [16, 14, 16, 16], P('seg'), may hold values from -4 to 4
- sector_map: int32 [16, 14, 4], P('seg'), may hold values from 0 to 3, as said below
- ranks: int32 [16, 4], P('seg', 'blk'), may hold values from 1 to 128
Outputs:
- new_state: bfloat16 [16, 4, 128, 2048], P('seg', 'blk')
- from_left: float32 [16, 14, 4, 128, 128], P('seg', None, 'blk')
- from_right: float32 [16, 14, 4, 128, 128], P('seg', None, 'blk')
Inputs may be any that keep to these rules, and one draw needn't show every extreme that they name: `sector_map`: channel 0 carries every block into itself; the other channels' source blocks are arbitrary.
All inputs are finite; a program needn't handle non-finite values.
Results may differ from a plain program's by a relative error of at most 0.012.
Values may be sent and summed in bfloat16 or wider, within the bound.
No kernel may reach another device: no remote copies, remote signals or barrier semaphores. Data moves between devices by JAX's collectives and lax.ppermute only.
A program may use at most 192 MiB of HBM per device.

v0:
```python
import functools
import math

import jax
import jax.numpy as jnp
from jax import lax
from jax.experimental import pallas as pl
from jax.experimental.pallas import tpu as pltpu
from jax.sharding import PartitionSpec as P

STEP_SIZE = 0.25
EPSILON = 1e-06
LANES = 128
ROWS = 16
F32 = jnp.float32
BF16 = jnp.bfloat16
VMEM = pl.BlockSpec(memory_space=pltpu.VMEM)
SMEM = pl.BlockSpec(memory_space=pltpu.SMEM)
PARAMS = pltpu.CompilerParams(vmem_limit_bytes=32 * 1024 * 1024)


def dot(left, right):
    return lax.dot_general(
        left, right, (((1,), (0,)), ((), ())), preferred_element_type=F32
    )


def make_kron(ops_ref, kron_ref):
    chan, phys, _ = ops_ref.shape
    wide = phys * ROWS
    spread_rows = (
        lax.broadcasted_iota(jnp.int32, (wide, phys), 0) // ROWS
        == lax.broadcasted_iota(jnp.int32, (wide, phys), 1)
    ).astype(F32).astype(BF16)
    spread_cols = (
        lax.broadcasted_iota(jnp.int32, (phys, wide), 1) // ROWS
        == lax.broadcasted_iota(jnp.int32, (phys, wide), 0)
    ).astype(F32).astype(BF16)
    diagonal = (
        lax.broadcasted_iota(jnp.int32, (wide, wide), 0) % ROWS
        == lax.broadcasted_iota(jnp.int32, (wide, wide), 1) % ROWS
    )

    def one(k, carry):
        tall = dot(spread_rows, ops_ref[k]).astype(BF16)
        full = dot(tall, spread_cols)
        kron_ref[k] = jnp.where(diagonal, full, 0.0).astype(BF16)
        return carry

    lax.fori_loop(0, chan, one, 0)


def list_pairs(rel_ref, low, high, chan_list, src_list, live_list, dest_list):
    chan, dests = rel_ref.shape
    place = jnp.int32(0)
    for b in range(dests):
        for k in range(chan):
            source = rel_ref[k, b]
            chan_list[place] = k
            src_list[place] = source - low
            live_list[place] = 1
            dest_list[place] = b
            place = place + jnp.where((source >= low) & (source < high), 1, 0)
        chan_list[place] = 0
        src_list[place] = 0
        live_list[place] = 0
        dest_list[place] = b
        place = place + lax.rem(place, 2)
    return place // 2


def add_pairs(steps, lists, kron_ref, x_ref, left_ref, right_t_ref, acc_ref, mixed_ref, part_ref):
    chan_list, src_list, live_list, dest_list = lists
    rows = x_ref.shape[1]
    phys = x_ref.shape[2] // LANES

    def step(s, carry):
        dest = dest_list[2 * s]
        weights = []
        for i in range(2):
            k = chan_list[2 * s + i]
            source = src_list[2 * s + i]
            kron = kron_ref[k]
            for g in range(rows // (2 * ROWS)):
                halves = []
                for j in range(2):
                    r0 = (2 * g + j) * ROWS
                    halves.append(
                        jnp.concatenate(
                            [
                                x_ref[source, r0 : r0 + ROWS, q * LANES : (q + 1) * LANES]
                                for q in range(phys)
                            ],
                            axis=0,
                        )
                    )
                out = dot(kron, jnp.concatenate(halves, axis=1)).astype(BF16)
                for j in range(2):
                    r0 = (2 * g + j) * ROWS
                    for p in range(phys):
                        mixed_ref[i, r0 : r0 + ROWS, p * LANES : (p + 1) * LANES] = out[
                            p * ROWS : (p + 1) * ROWS, j * LANES : (j + 1) * LANES
                        ]
            left = left_ref[k, dest]
            for c in range(phys // 2):
                cols = slice(c * 2 * LANES, (c + 1) * 2 * LANES)
                part_ref[i, :, cols] = dot(left, mixed_ref[i, :, cols]).astype(BF16)
            right = right_t_ref[k, dest]
            if i == 1:
                right = jnp.where(live_list[2 * s + 1] > 0, right, jnp.zeros_like(right))
            weights.append(right)
        both = jnp.concatenate(weights, axis=0)
        for p in range(phys):
            cols = slice(p * LANES, (p + 1) * LANES)
            pair = jnp.concatenate([part_ref[0, :, cols], part_ref[1, :, cols]], axis=1)
            acc_ref[dest, :, cols] += dot(pair, both)
        return carry

    lax.fori_loop(0, steps, step, 0)


def fold(values):
    total = values[:, :LANES]
    for p in range(1, values.shape[1] // LANES):
        total = total + values[:, p * LANES : (p + 1) * LANES]
    return total


def row_loop(blocks, rows, body, count):
    zeros = tuple(jnp.zeros((ROWS, LANES), F32) for _ in range(count))
    per = rows // ROWS

    def step(n, carry):
        return body(n // per, pl.ds(pl.multiple_of(lax.rem(n, per) * ROWS, ROWS), ROWS), carry)

    return lax.fori_loop(0, blocks * per, step, zeros)


def put_sums(out_ref, values):
    for n, value in enumerate(values):
        out_ref[n : n + 1, :] = jnp.full((1, LANES), 1.0, F32) * value


def quotient(num, den):
    return jnp.where(den > 0, num / jnp.where(den > 0, den, 1.0), 0.0)


def first_local(
    rel_ref, ops_ref, x_ref, left_ref, right_ref,
    kron_ref, right_t_ref, image_ref, sums_ref,
    mixed_ref, part_ref, chan_list, src_list, live_list, dest_list,
):
    lists = (chan_list, src_list, live_list, dest_list)
    make_kron(ops_ref, kron_ref)
    chan, dests = left_ref.shape[:2]

    def turn(n, carry):
        k, b = n // dests, lax.rem(n, dests)
        right_t_ref[k, b] = right_ref[k, b].astype(F32).T.astype(BF16)
        return carry

    lax.fori_loop(0, chan * dests, turn, 0)
    image_ref[...] = jnp.zeros_like(image_ref)
    steps = list_pairs(rel_ref, 0, dests, *lists)
    add_pairs(steps, lists, kron_ref, x_ref, left_ref, right_t_ref, image_ref, mixed_ref, part_ref)

    def sums(b, r, carry):
        x = x_ref[b, r, :].astype(F32)
        return carry[0] + fold(x * image_ref[b, r, :]), carry[1] + fold(x * x)

    num, den = row_loop(dests, x_ref.shape[1], sums, 2)
    put_sums(sums_ref, (jnp.sum(num), jnp.sum(den)))


def first_remote(
    rel_ref, kron_ref, other_ref, left_ref, right_t_ref,
    acc_ref,
    mixed_ref, part_ref, chan_list, src_list, live_list, dest_list,
):
    lists = (chan_list, src_list, live_list, dest_list)
    dests = left_ref.shape[1]
    acc_ref[...] = jnp.zeros_like(acc_ref)
    steps = list_pairs(rel_ref, dests, dests + 1, *lists)
    add_pairs(steps, lists, kron_ref, other_ref, left_ref, right_t_ref, acc_ref, mixed_ref, part_ref)


def first_finish(
    rel_ref, kron_ref, other_ref, left_ref, right_t_ref, before_ref, x_ref, image_ref, sums_ref,
    acc_ref, guess_ref, out_sums_ref,
    mixed_ref, part_ref, chan_list, src_list, live_list, dest_list,
):
    lists = (chan_list, src_list, live_list, dest_list)
    dests = left_ref.shape[1]
    acc_ref[...] = before_ref[...]
    steps = list_pairs(rel_ref, dests + 1, 2 * dests, *lists)
    add_pairs(steps, lists, kron_ref, other_ref, left_ref, right_t_ref, acc_ref, mixed_ref, part_ref)
    num_local, den = sums_ref[0:1, :], sums_ref[1:2, :]
    shift = quotient(num_local, den)
    keep_state = jnp.tile(1.0 + STEP_SIZE * shift, (1, x_ref.shape[2] // LANES))

    def sums(b, r, carry):
        x = x_ref[b, r, :].astype(F32)
        remote = acc_ref[b, r, :]
        guess_ref[b, r, :] = (keep_state * x - STEP_SIZE * (image_ref[b, r, :] + remote)).astype(BF16)
        return (carry[0] + fold(x * remote),)

    (num,) = row_loop(dests, x_ref.shape[1], sums, 1)
    out_sums_ref[0:1, :] = num_local + jnp.sum(num)
    out_sums_ref[1:2, :] = den
    out_sums_ref[2:3, :] = shift
    out_sums_ref[3:8, :] = jnp.zeros((5, LANES), F32)


def second_local(
    rel_ref, kron_ref, guess_ref, left_ref, right_t_ref,
    acc_ref,
    mixed_ref, part_ref, chan_list, src_list, live_list, dest_list,
):
    lists = (chan_list, src_list, live_list, dest_list)
    dests = left_ref.shape[1]
    acc_ref[...] = jnp.zeros_like(acc_ref)
    steps = list_pairs(rel_ref, 0, dests, *lists)
    add_pairs(steps, lists, kron_ref, guess_ref, left_ref, right_t_ref, acc_ref, mixed_ref, part_ref)


def second_remote(
    rel_ref, kron_ref, other_ref, left_ref, right_t_ref, before_ref, x_ref, image_ref, remote_ref,
    mine_ref, theirs_ref,
    acc_ref, first_ref,
    mixed_ref, part_ref, chan_list, src_list, live_list, dest_list,
):
    lists = (chan_list, src_list, live_list, dest_list)
    dests = left_ref.shape[1]
    energy = (mine_ref[0:1, :] + theirs_ref[0:1, :]) / (mine_ref[1:2, :] + theirs_ref[1:2, :])
    times = x_ref.shape[2] // LANES
    wide = functools.partial(jnp.tile, reps=(1, times))
    keep_state = wide(1.0 + STEP_SIZE * energy)
    scale_local = wide(STEP_SIZE * (energy - mine_ref[2:3, :]))
    scale_remote = wide(STEP_SIZE * (energy - theirs_ref[2:3, :]))

    def prepare(b, r, carry):
        local, remote = image_ref[b, r, :], remote_ref[b, r, :]
        x = x_ref[b, r, :].astype(F32)
        first_ref[b, r, :] = (keep_state * x - STEP_SIZE * (local + remote)).astype(BF16)
        acc_ref[b, r, :] = before_ref[b, r, :] + (scale_local * local + scale_remote * remote)
        return carry

    row_loop(dests, x_ref.shape[1], prepare, 0)
    steps = list_pairs(rel_ref, dests, dests + 1, *lists)
    add_pairs(steps, lists, kron_ref, other_ref, left_ref, right_t_ref, acc_ref, mixed_ref, part_ref)


def second_finish(
    rel_ref, rank_ref, kron_ref, other_ref, left_ref, right_t_ref, before_ref, first_ref,
    mine_ref, theirs_ref,
    kept_ref, kept_first_ref, out_sums_ref,
    acc_ref, mixed_ref, part_ref, chan_list, src_list, live_list, dest_list,
):
    lists = (chan_list, src_list, live_list, dest_list)
    dests = left_ref.shape[1]
    acc_ref[...] = before_ref[...]
    steps = list_pairs(rel_ref, dests + 1, 2 * dests, *lists)
    add_pairs(steps, lists, kron_ref, other_ref, left_ref, right_t_ref, acc_ref, mixed_ref, part_ref)
    energy = (mine_ref[0:1, :] + theirs_ref[0:1, :]) / (mine_ref[1:2, :] + theirs_ref[1:2, :])
    width = first_ref.shape[2]
    keep_first = jnp.tile(1.0 + STEP_SIZE * energy, (1, width // LANES))

    def sums(b, r, carry):
        first = first_ref[b, r, :].astype(F32)
        image = acc_ref[b, r, :]
        row = r.start + lax.broadcasted_iota(jnp.int32, (ROWS, width), 0)
        mask = row < rank_ref[b]
        kept = jnp.where(mask, keep_first * first - STEP_SIZE * image, 0.0)
        kept_first = jnp.where(mask, first, 0.0)
        kept_ref[b, r, :] = kept
        kept_first_ref[b, r, :] = kept_first.astype(BF16)
        return (
            carry[0] + fold(first * image),
            carry[1] + fold(first * first),
            carry[2] + fold(kept * kept),
            carry[3] + fold(kept * first),
            carry[4] + fold(kept_first * first),
        )

    totals = row_loop(dests, first_ref.shape[1], sums, 5)
    for n, total in enumerate(totals):
        out_sums_ref[n : n + 1, :] = jnp.full((1, LANES), 1.0, F32) * jnp.sum(total)
    out_sums_ref[5:6, :] = energy
    out_sums_ref[6:8, :] = jnp.zeros((2, LANES), F32)


def normalize(
    cells, kept_ref, first_ref, mine_ref, theirs_ref, state_ref, turned_ref,
):
    both = mine_ref[...] + theirs_ref[...]
    shift = STEP_SIZE * (both[0:1] / both[1:2] - mine_ref[5:6, :])
    norm = jnp.maximum(both[2:3] + shift * (2.0 * both[3:4] + shift * both[4:5]), 0.0)
    gain = jnp.sqrt(cells / (norm + EPSILON))
    times = kept_ref.shape[2] // LANES
    gain, shift = jnp.tile(gain, (1, times)), jnp.tile(shift, (1, times))

    def one(b, r, carry):
        state_ref[b, r, :] = (
            (kept_ref[b, r, :] + shift * first_ref[b, r, :].astype(F32)) * gain
        ).astype(BF16)
        return carry

    blocks, rows, _ = kept_ref.shape
    row_loop(blocks, rows, one, 0)

    def turn(n, carry):
        b, p = n // times, lax.rem(n, times)
        cols = pl.ds(pl.multiple_of(p * LANES, LANES), LANES)
        turned_ref[b, :, cols] = state_ref[b, :, cols].astype(F32).T.astype(BF16)
        return carry

    lax.fori_loop(0, blocks * times, turn, 0)


def environments(first, count, scale, env_ref, inner_ref, outer_ref, out_ref, mid_ref):
    dests = env_ref.shape[1]
    phys = inner_ref.shape[2] // LANES

    def step(n, carry):
        pair, b = n // dests, lax.rem(n, dests)
        k = first + 2 * pair
        env = jnp.concatenate([env_ref[k, b], env_ref[k + 1, b]], axis=0)
        for c in range(phys // 2):
            cols = slice(c * 2 * LANES, (c + 1) * 2 * LANES)
            mid = dot(env, inner_ref[b, :, cols]).astype(BF16)
            for h in range(2):
                p = 2 * c + h
                for i in range(2):
                    mid_ref[p * LANES : (p + 1) * LANES, i * LANES : (i + 1) * LANES] = mid[
                        i * LANES : (i + 1) * LANES, h * LANES : (h + 1) * LANES
                    ]
        out = (dot(outer_ref[b], mid_ref[...]) * scale).astype(BF16)
        out_ref[2 * pair, b] = out[:, :LANES]
        out_ref[2 * pair + 1, b] = out[:, LANES:]
        return carry

    lax.fori_loop(0, (count // 2) * dests, step, 0)


def normalize_and_left(
    first, count, scale, cells,
    kept_ref, first_ref, mine_ref, theirs_ref, env_ref,
    state_ref, turned_ref, out_ref,
    mid_ref,
):
    normalize(cells, kept_ref, first_ref, mine_ref, theirs_ref, state_ref, turned_ref)
    environments(first, count, scale, env_ref, state_ref, turned_ref, out_ref, mid_ref)


def shards(state, left_env, right_env, site_ops, sector_map, ranks):
    dests, rows, width = state.shape[1:]
    chan, phys = site_ops.shape[1:3]
    groups = lax.axis_size("blk")
    total_blocks = groups * dests
    first_block = lax.axis_index("blk") * dests
    x, left, right, ops = state[0], left_env[0], right_env[0], site_ops[0]
    local_map = lax.dynamic_slice_in_dim(sector_map[0], first_block, dests, 1)
    rel = lax.rem(local_map - first_block + total_blocks, total_blocks)

    swap = [(g, groups - 1 - g) for g in range(groups)]

    def trade(value):
        return lax.ppermute(value, "blk", swap)

    def shape(dims, kind):
        return jax.ShapeDtypeStruct(dims, kind)

    wave = (dests, rows, width)
    wave_f32 = shape(wave, F32)
    wave_b16 = shape(wave, BF16)
    sums_kind = shape((8, LANES), F32)
    lists = [pltpu.SMEM((chan * dests + 2 * dests + 1,), jnp.int32)] * 4
    pair_scratch = [pltpu.VMEM((2, rows, width), BF16)] * 2 + lists
    one_apply = 2 * chan * dests * rows * width * (ROWS * phys + 2 * rows)

    def call(body, specs, outs, scratch, share, *args):
        return pl.pallas_call(
            body,
            in_specs=specs,
            out_specs=jax.tree.map(lambda _: VMEM, outs),
            out_shape=outs,
            scratch_shapes=scratch,
            compiler_params=PARAMS,
            cost_estimate=pl.CostEstimate(
                flops=int(one_apply * share), bytes_accessed=8 * 1024 * 1024, transcendentals=0
            ),
        )(*args)

    other = [trade(x[b : b + 1]) for b in range(dests)]
    kron, right_t, image_local, sums_local = call(
        first_local, [SMEM] + [VMEM] * 4,
        (shape((chan, phys * ROWS, phys * ROWS), BF16), shape(right.shape, BF16), wave_f32, sums_kind),
        pair_scratch, 0.7, rel, ops, x, left, right,
    )
    image_remote = call(
        first_remote, [SMEM] + [VMEM] * 4, wave_f32, pair_scratch, 0.25,
        rel, kron, other[0], left, right_t,
    )
    image_remote, guess, mine = call(
        first_finish, [SMEM] + [VMEM] * 8, (wave_f32, wave_b16, sums_kind), pair_scratch, 0.3,
        rel, kron, other[1], left, right_t, image_remote, x, image_local, sums_local,
    )
    theirs = trade(mine)
    other = [trade(guess[b : b + 1]) for b in range(dests)]
    acc = call(
        second_local, [SMEM] + [VMEM] * 4, wave_f32, pair_scratch, 0.5,
        rel, kron, guess, left, right_t,
    )
    acc, first = call(
        second_remote, [SMEM] + [VMEM] * 10, (wave_f32, wave_b16), pair_scratch, 0.25,
        rel, kron, other[0], left, right_t, acc, x, image_local, image_remote, mine, theirs,
    )
    kept, kept_first, sums_mine = call(
        second_finish, [SMEM, SMEM] + [VMEM] * 8, (wave_f32, wave_b16, sums_kind),
        [pltpu.VMEM(wave, F32)] + pair_scratch, 0.3,
        rel, ranks[0], kron, other[1], left, right_t, acc, first, mine, theirs,
    )
    sums_theirs = trade(sums_mine)

    env_scale = 1.0 / math.sqrt(phys * rows)
    cells = float(total_blocks * rows * width)
    half = chan // 4 * 2
    cuts = [(0, half), (half, chan - half)]
    mid = [pltpu.VMEM((width, 2 * LANES), BF16)]

    def sent(value, steps):
        count = lax.axis_size("seg")
        begin, end = max(0, -steps), min(count, count - steps)
        return lax.ppermute(value, "seg", [(s, s + steps) for s in range(begin, end)])

    def env_kind(count):
        return shape((count,) + left.shape[1:], BF16)

    lefts, rights = [], []
    for n, (begin, count) in enumerate(cuts):
        if n == 0:
            new_state, turned, piece = call(
                functools.partial(normalize_and_left, begin, count, env_scale, cells),
                [VMEM] * 5, (wave_b16, wave_b16, env_kind(count)), mid, 0.3,
                kept, kept_first, sums_mine, sums_theirs, left,
            )
        else:
            piece = call(
                functools.partial(environments, begin, count, env_scale),
                [VMEM] * 3, env_kind(count), mid, 0.3, left, new_state, turned,
            )
        lefts.append(sent(piece, 1))
        piece = call(
            functools.partial(environments, begin, count, env_scale),
            [VMEM] * 3, env_kind(count), mid, 0.3, right, turned, new_state,
        )
        rights.append(sent(piece, -1))
    received_left = jnp.concatenate(lefts, axis=0).astype(F32)
    received_right = jnp.concatenate(rights, axis=0).astype(F32)
    return (new_state[None], received_left[None], received_right[None])


def solution(mesh):
    placed = (
        P("seg", "blk", None, None),
        P("seg", None, "blk", None, None),
        P("seg", None, "blk", None, None),
        P("seg", None, None, None),
        P("seg", None, None),
        P("seg", "blk"),
    )
    return jax.shard_map(
        shards,
        mesh=mesh,
        in_specs=placed,
        out_specs=(
            P("seg", "blk", None, None),
            P("seg", None, "blk", None, None),
            P("seg", None, "blk", None, None),
        ),
        check_vma=False,
    )
```

profile of v0, /device:TPU:16, one launch (start us, length us, event | category | flops | bytes accessed | tf_op | source)
XLA Modules:
  0.0 123.9 jit_solution(15272505531704312827)
XLA Ops:
  0.6 0.0 copy-start
  0.6 0.0 copy-start.7
  0.7 0.0 copy-start.4
  0.7 0.0 copy-start.1
  0.7 2.4 %slice_bitcast_fusion = (bf16[1,128,2048]{2,1,0:T(8,128)(2,1)}, bf16[1,128,2048]{2,1,0:T(8,128)(2,1)}) fusion(bf16[1,2,128,2048]{3,2,1,0:T(8,128)(2,1)} %param.6), kind=kLoop, calls=%fused_computation.2 | loop fusion | bytes 2097152 | tf_op jit(solution)/shard_map/slice | solution.py:394
  3.1 1.5 %collective-permute-start.1 = (bf16[1,128,2048]{2,1,0:T(8,128)(2,1)}, bf16[1,128,2048]{2,1,0:T(8,128)(2,1)S(1)}, u32[]{:S(2)}, u32[]{:S(2)}) collective-permute-start(bf16[1,128,2048]{2,1,0:T(8,128)(2,1)} %get-tuple-element.35), channel_id=1, source_target_pairs={{0,1},{1,0},{2,3},{3,2},{4,5},{5,4},{6,7},{7,6},{8,9},{9,8},{10,11... | collective-permute-start | bytes 1572872 | tf_op jit(solution)/shard_map/ppermute | solution.py:368
  4.6 0.5 collective-permute-start
  5.1 0.0 copy-done.7
  5.1 0.1 copy.9
  5.2 0.0 copy-done
  5.2 0.0 copy-done.4
  5.2 0.0 copy-done.1
  5.2 0.0 copy-start.2
  5.3 1.2 copy-done.2
  6.4 18.4 %shard_map.85 = (bf16[14,256,256]{2,1,0:T(8,128)(2,1)S(1)}, bf16[14,2,128,128]{3,2,1,0:T(8,128)(2,1)S(1)}, f32[2,128,2048]{2,1,0:T(8,128)S(1)}, f32[8,128]{1,0:T(8,128)S(1)}) custom-call(s32[14,2]{1,0:T(8,128)S(1)} %negate_select_fusion.rel_ref, bf16[14,16,16]{2,1,0:T(8,128)(2,1)S(1)} %bitcast.30, bf16[2,128,2048]{2,1,0:T(8,128)(2,1)S(1)} %bitcast.16, ...), custom_call_target="tpu_custom_call" | custom-call | flops 5261335040 | bytes 8388608 | tf_op jit(solution)/shard_map/pallas_call | solution.py:382
  24.8 0.0 collective-permute-done.1.other_ref
  24.9 4.4 %shard_map.86.before_ref = f32[2,128,2048]{2,1,0:T(8,128)S(1)} custom-call(s32[14,2]{1,0:T(8,128)S(1)} %negate_select_fusion.rel_ref, bf16[14,256,256]{2,1,0:T(8,128)(2,1)S(1)} %get-tuple-element.18.kron_ref, bf16[1,128,2048]{2,1,0:T(8,128)(2,1)S(1)} %collective-permute-done.1.other_ref, bf16[14,2,128,128]{3,2,1,0:T(8,128)(2,1)S(1)} %bitcast.20, ...), custom_call_target="tpu_custom_call" | custom-call | flops 1879048192 | bytes 8388608 | tf_op jit(solution)/shard_map/pallas_call | solution.py:382
  29.3 0.0 collective-permute-done.other_ref
  29.3 7.7 %shard_map.87 = (f32[2,128,2048]{2,1,0:T(8,128)S(1)}, bf16[2,128,2048]{2,1,0:T(8,128)(2,1)S(1)}, f32[8,128]{1,0:T(8,128)S(1)}) custom-call(s32[14,2]{1,0:T(8,128)S(1)} %negate_select_fusion.rel_ref, bf16[14,256,256]{2,1,0:T(8,128)(2,1)S(1)} %get-tuple-element.18.kron_ref, bf16[1,128,2048]{2,1,0:T(8,128)(2,1)S(1)} %collective-permute-done.other_ref, ...), custom_call_target="tpu_custom_call" | custom-call | flops 2254857728 | bytes 8388608 | tf_op jit(solution)/shard_map/pallas_call | solution.py:382
  37.0 0.1 fusion.1
  37.1 0.4 collective-permute-start.3
  37.5 1.7 %collective-permute-start.4 = (f32[8,128]{1,0:T(8,128)S(1)}, f32[8,128]{1,0:T(8,128)S(1)}, u32[]{:S(2)}, u32[]{:S(2)}) collective-permute-start(f32[8,128]{1,0:T(8,128)S(1)} %get-tuple-element.24.mine_ref), channel_id=1, source_target_pairs={{0,1},{1,0},{2,3},{3,2},{4,5},{5,4},{6,7},{7,6},{8,9},{9,8},{10,11... | collective-permute-start | bytes 12296 | tf_op jit(solution)/shard_map/ppermute | solution.py:368
  39.2 0.3 collective-permute-start.2
  39.5 10.5 %shard_map.88.before_ref = f32[2,128,2048]{2,1,0:T(8,128)S(1)} custom-call(s32[14,2]{1,0:T(8,128)S(1)} %negate_select_fusion.rel_ref, bf16[14,256,256]{2,1,0:T(8,128)(2,1)S(1)} %get-tuple-element.18.kron_ref, bf16[2,128,2048]{2,1,0:T(8,128)(2,1)S(1)} %get-tuple-element.22.guess_ref, bf16[14,2,128,128]{3,2,1,0:T(8,128)(2,1)S(1)} %bitcast.22, ...), custom_call_target="tpu_custom_call" | custom-call | flops 3758096384 | bytes 8388608 | tf_op jit(solution)/shard_map/pallas_call | solution.py:382
  50.0 2.1 %collective-permute-done.4.theirs_ref = f32[8,128]{1,0:T(8,128)S(1)} collective-permute-done((f32[8,128]{1,0:T(8,128)S(1)}, f32[8,128]{1,0:T(8,128)S(1)}, u32[]{:S(2)}, u32[]{:S(2)}) %collective-permute-start.4) | collective-permute-done | bytes 4128 | tf_op jit(solution)/shard_map/ppermute | solution.py:368
  52.1 0.0 collective-permute-done.3.other_ref
  52.2 0.0 copy-start.5
  52.2 5.3 %shard_map.89 = (f32[2,128,2048]{2,1,0:T(8,128)S(1)}, bf16[2,128,2048]{2,1,0:T(8,128)(2,1)S(1)}) custom-call(s32[14,2]{1,0:T(8,128)S(1)} %negate_select_fusion.rel_ref, bf16[14,256,256]{2,1,0:T(8,128)(2,1)S(1)} %get-tuple-element.18.kron_ref, bf16[1,128,2048]{2,1,0:T(8,128)(2,1)S(1)} %collective-permute-done.3.other_ref, ...), custom_call_target="tpu_custom_call" | custom-call | flops 1879048192 | bytes 8388608 | tf_op jit(solution)/shard_map/pallas_call | solution.py:382
  57.4 4.2 %collective-permute-done.2.other_ref = bf16[1,128,2048]{2,1,0:T(8,128)(2,1)S(1)} collective-permute-done((bf16[1,128,2048]{2,1,0:T(8,128)(2,1)S(1)}, bf16[1,128,2048]{2,1,0:T(8,128)(2,1)S(1)}, u32[]{:S(2)}, u32[]{:S(2)}) %collective-permute-start.2) | collective-permute-done | bytes 524320 | tf_op jit(solution)/shard_map/ppermute | solution.py:368
  61.7 0.0 copy-done.5
  61.7 8.4 %shard_map.90 = (f32[2,128,2048]{2,1,0:T(8,128)S(1)}, bf16[2,128,2048]{2,1,0:T(8,128)(2,1)S(1)}, f32[8,128]{1,0:T(8,128)S(1)}) custom-call(s32[14,2]{1,0:T(8,128)S(1)} %negate_select_fusion.rel_ref, s32[2]{0:T(128)S(1)} %bitcast.31, bf16[14,256,256]{2,1,0:T(8,128)(2,1)S(1)} %get-tuple-element.18.kron_ref, ...), custom_call_target="tpu_custom_call" | custom-call | flops 2254857728 | bytes 8388608 | tf_op jit(solution)/shard_map/pallas_call | solution.py:382
  70.1 0.1 collective-permute-start.5
  70.2 3.6 %collective-permute-done.5.theirs_ref = f32[8,128]{1,0:T(8,128)S(1)} collective-permute-done((f32[8,128]{1,0:T(8,128)S(1)}, f32[8,128]{1,0:T(8,128)S(1)}, u32[]{:S(2)}, u32[]{:S(2)}) %collective-permute-start.5) | collective-permute-done | bytes 4128 | tf_op jit(solution)/shard_map/ppermute | solution.py:368
  73.8 0.0 copy-start.3
  73.8 9.0 %shard_map.91 = (bf16[2,128,2048]{2,1,0:T(8,128)(2,1)}, bf16[2,128,2048]{2,1,0:T(8,128)(2,1)S(1)}, bf16[6,2,128,128]{3,2,1,0:T(8,128)(2,1)S(1)}) custom-call(f32[2,128,2048]{2,1,0:T(8,128)S(1)} %get-tuple-element.27.kept_ref, bf16[2,128,2048]{2,1,0:T(8,128)(2,1)S(1)} %get-tuple-element.28.first_ref, f32[8,128]{1,0:T(8,128)S(1)} %get-tuple-element.29.mine_ref, ...), custom_call_target="tpu_custom_call" | custom-call | flops 2254857728 | bytes 8388608 | tf_op jit(solution)/shard_map/pallas_call | solution.py:382
  82.7 0.0 copy-done.3
  82.7 0.0 copy-start.6
  82.7 1.2 copy-done.6
  84.0 4.9 %shard_map.93 = bf16[6,2,128,128]{3,2,1,0:T(8,128)(2,1)S(1)} custom-call(bf16[14,2,128,128]{3,2,1,0:T(8,128)(2,1)S(1)} %bitcast.28, bf16[2,128,2048]{2,1,0:T(8,128)(2,1)S(1)} %get-tuple-element.32.outer_ref.inner_ref, bf16[2,128,2048]{2,1,0:T(8,128)(2,1)S(1)} %copy-done.6), custom_call_target="tpu_custom_call" | custom-call | flops 2254857728 | bytes 8388608 | tf_op jit(solution)/shard_map/pallas_call | solution.py:382
  88.8 6.5 %shard_map.94 = bf16[8,2,128,128]{3,2,1,0:T(8,128)(2,1)S(1)} custom-call(bf16[14,2,128,128]{3,2,1,0:T(8,128)(2,1)S(1)} %bitcast.29, bf16[2,128,2048]{2,1,0:T(8,128)(2,1)S(1)} %get-tuple-element.32.outer_ref.inner_ref, bf16[2,128,2048]{2,1,0:T(8,128)(2,1)S(1)} %copy-done.6), custom_call_target="tpu_custom_call" | custom-call | flops 2254857728 | bytes 8388608 | tf_op jit(solution)/shard_map/pallas_call | solution.py:382
  95.4 1.9 %collective-permute-start.8 = (bf16[6,2,128,128]{3,2,1,0:T(8,128)(2,1)S(1)}, bf16[6,2,128,128]{3,2,1,0:T(8,128)(2,1)S(1)}, u32[]{:S(2)}, u32[]{:S(2)}) collective-permute-start(bf16[6,2,128,128]{3,2,1,0:T(8,128)(2,1)S(1)} %shard_map.93), channel_id=1, source_target_pairs={{2,0},{4,2},{6,4},{8,6},{10,8},{12,10},{14,12},{16,14},{18,16},{20... | collective-permute-start | bytes 1179656 | tf_op jit(solution)/shard_map/ppermute | solution.py:434
  97.3 3.1 %collective-permute-start.9 = (bf16[8,2,128,128]{3,2,1,0:T(8,128)(2,1)S(1)}, bf16[8,2,128,128]{3,2,1,0:T(8,128)(2,1)S(1)}, u32[]{:S(2)}, u32[]{:S(2)}) collective-permute-start(bf16[8,2,128,128]{3,2,1,0:T(8,128)(2,1)S(1)} %shard_map.94), channel_id=1, source_target_pairs={{2,0},{4,2},{6,4},{8,6},{10,8},{12,10},{14,12},{16,14},{18,16},{20... | collective-permute-start | bytes 1572872 | tf_op jit(solution)/shard_map/ppermute | solution.py:434
  100.4 6.5 %shard_map.92 = bf16[8,2,128,128]{3,2,1,0:T(8,128)(2,1)S(1)} custom-call(bf16[14,2,128,128]{3,2,1,0:T(8,128)(2,1)S(1)} %bitcast.26, bf16[2,128,2048]{2,1,0:T(8,128)(2,1)S(1)} %copy-done.6, bf16[2,128,2048]{2,1,0:T(8,128)(2,1)S(1)} %get-tuple-element.32.outer_ref.inner_ref), custom_call_target="tpu_custom_call" | custom-call | flops 2254857728 | bytes 8388608 | tf_op jit(solution)/shard_map/pallas_call | solution.py:382
  107.0 1.9 %collective-permute-start.7 = (bf16[8,2,128,128]{3,2,1,0:T(8,128)(2,1)S(1)}, bf16[8,2,128,128]{3,2,1,0:T(8,128)(2,1)S(1)}, u32[]{:S(2)}, u32[]{:S(2)}) collective-permute-start(bf16[8,2,128,128]{3,2,1,0:T(8,128)(2,1)S(1)} %shard_map.92), channel_id=1, source_target_pairs={{0,2},{2,4},{4,6},{6,8},{8,10},{10,12},{12,14},{14,16},{16,18},{18... | collective-permute-start | bytes 1572872 | tf_op jit(solution)/shard_map/ppermute | solution.py:434
  108.9 3.0 %collective-permute-start.6 = (bf16[6,2,128,128]{3,2,1,0:T(8,128)(2,1)S(1)}, bf16[6,2,128,128]{3,2,1,0:T(8,128)(2,1)S(1)}, u32[]{:S(2)}, u32[]{:S(2)}) collective-permute-start(bf16[6,2,128,128]{3,2,1,0:T(8,128)(2,1)S(1)} %get-tuple-element.31), channel_id=1, source_target_pairs={{0,2},{2,4},{4,6},{6,8},{8,10},{10,12},{12,14},{14,16},{16,18},{18... | collective-permute-start | bytes 1179656 | tf_op jit(solution)/shard_map/ppermute | solution.py:434
  111.9 0.0 collective-permute-done.8
  112.0 0.0 collective-permute-done.9
  112.0 1.4 %maximum_convert_fusion.1 = f32[1,14,2,128,128]{4,3,2,1,0:T(8,128)} fusion(bf16[1,8,2,128,128]{4,3,2,1,0:T(8,128)(2,1)S(1)} %bitcast.34, bf16[1,6,2,128,128]{4,3,2,1,0:T(8,128)(2,1)S(1)} %bitcast.35), kind=kLoop, calls=%fused_computation.1 | loop fusion | flops 917504 | bytes 2752512 | tf_op jit(solution)/shard_map/convert_element_type | solution.py:459
  113.3 9.3 %collective-permute-done.6 = bf16[6,2,128,128]{3,2,1,0:T(8,128)(2,1)S(1)} collective-permute-done((bf16[6,2,128,128]{3,2,1,0:T(8,128)(2,1)S(1)}, bf16[6,2,128,128]{3,2,1,0:T(8,128)(2,1)S(1)}, u32[]{:S(2)}, u32[]{:S(2)}) %collective-permute-start.6) | collective-permute-done | bytes 393248 | tf_op jit(solution)/shard_map/ppermute | solution.py:434
  122.6 0.0 collective-permute-done.7
  122.6 1.4 %maximum_convert_fusion = f32[1,14,2,128,128]{4,3,2,1,0:T(8,128)} fusion(bf16[1,8,2,128,128]{4,3,2,1,0:T(8,128)(2,1)S(1)} %bitcast.33, bf16[1,6,2,128,128]{4,3,2,1,0:T(8,128)(2,1)S(1)} %bitcast.36), kind=kLoop, calls=%fused_computation | loop fusion | flops 917504 | bytes 2752512 | tf_op jit(solution)/shard_map/convert_element_type | solution.py:458
  (2 shorter events, 0.0 us)
Async XLA Ops:
  0.6 4.6 %copy-start = (bf16[1,2,128,2048]{3,2,1,0:T(8,128)(2,1)S(1)}, bf16[1,2,128,2048]{3,2,1,0:T(8,128)(2,1)}, u32[]{:S(2)}) copy-start(bf16[1,2,128,2048]{3,2,1,0:T(8,128)(2,1)} %param.6) | copy-start | bytes 3145732
  0.6 4.5 %copy-start.7 = (s32[1,14,4]{1,2,0:T(4,128)S(1)}, s32[1,14,4]{1,2,0:T(4,128)}, u32[]{:S(2)}) copy-start(s32[1,14,4]{1,2,0:T(4,128)} %param.10) | copy-start | bytes 676
  0.7 4.6 %copy-start.4 = (bf16[1,14,16,16]{3,2,1,0:T(8,128)(2,1)S(1)}, bf16[1,14,16,16]{3,2,1,0:T(8,128)(2,1)}, u32[]{:S(2)}) copy-start(bf16[1,14,16,16]{3,2,1,0:T(8,128)(2,1)} %param.9) | copy-start | bytes 21508
  0.7 4.6 %copy-start.1 = (bf16[1,14,2,128,128]{4,3,2,1,0:T(8,128)(2,1)S(1)}, bf16[1,14,2,128,128]{4,3,2,1,0:T(8,128)(2,1)}, u32[]{:S(2)}) copy-start(bf16[1,14,2,128,128]{4,3,2,1,0:T(8,128)(2,1)} %param.7) | copy-start | bytes 2752516
  3.1 21.8 %collective-permute-start.1 = (bf16[1,128,2048]{2,1,0:T(8,128)(2,1)}, bf16[1,128,2048]{2,1,0:T(8,128)(2,1)S(1)}, u32[]{:S(2)}, u32[]{:S(2)}) collective-permute-start(bf16[1,128,2048]{2,1,0:T(8,128)(2,1)} %get-tuple-element.35), channel_id=1, source_target_pairs={{0,1},{1,0},{2,3},{3,2},{4,5},{5,4},{6,7},{7,6},{8,9},{9,8},{10,11... | collective-permute-start | bytes 1572872 | tf_op jit(solution)/shard_map/ppermute | solution.py:368
  4.6 24.7 %collective-permute-start = (bf16[1,128,2048]{2,1,0:T(8,128)(2,1)}, bf16[1,128,2048]{2,1,0:T(8,128)(2,1)S(1)}, u32[]{:S(2)}, u32[]{:S(2)}) collective-permute-start(bf16[1,128,2048]{2,1,0:T(8,128)(2,1)} %get-tuple-element.36), channel_id=1, source_target_pairs={{0,1},{1,0},{2,3},{3,2},{4,5},{5,4},{6,7},{7,6},{8,9},{9,8},{10,11... | collective-permute-start | bytes 1572872 | tf_op jit(solution)/shard_map/ppermute | solution.py:368
  5.2 1.2 copy-start.2
  37.1 15.0 %collective-permute-start.3 = (bf16[1,128,2048]{2,1,0:T(8,128)(2,1)S(1)}, bf16[1,128,2048]{2,1,0:T(8,128)(2,1)S(1)}, u32[]{:S(2)}, u32[]{:S(2)}) collective-permute-start(bf16[1,128,2048]{2,1,0:T(8,128)(2,1)S(1)} %get-tuple-element.33), channel_id=1, source_target_pairs={{0,1},{1,0},{2,3},{3,2},{4,5},{5,4},{6,7},{7,6},{8,9},{9,8},{10,11... | collective-permute-start | bytes 1572872 | tf_op jit(solution)/shard_map/ppermute | solution.py:368
  37.5 14.7 %collective-permute-start.4 = (f32[8,128]{1,0:T(8,128)S(1)}, f32[8,128]{1,0:T(8,128)S(1)}, u32[]{:S(2)}, u32[]{:S(2)}) collective-permute-start(f32[8,128]{1,0:T(8,128)S(1)} %get-tuple-element.24.mine_ref), channel_id=1, source_target_pairs={{0,1},{1,0},{2,3},{3,2},{4,5},{5,4},{6,7},{7,6},{8,9},{9,8},{10,11... | collective-permute-start | bytes 12296 | tf_op jit(solution)/shard_map/ppermute | solution.py:368
  39.2 22.4 %collective-permute-start.2 = (bf16[1,128,2048]{2,1,0:T(8,128)(2,1)S(1)}, bf16[1,128,2048]{2,1,0:T(8,128)(2,1)S(1)}, u32[]{:S(2)}, u32[]{:S(2)}) collective-permute-start(bf16[1,128,2048]{2,1,0:T(8,128)(2,1)S(1)} %get-tuple-element.34), channel_id=1, source_target_pairs={{0,1},{1,0},{2,3},{3,2},{4,5},{5,4},{6,7},{7,6},{8,9},{9,8},{10,11... | collective-permute-start | bytes 1572872 | tf_op jit(solution)/shard_map/ppermute | solution.py:368
  52.2 9.5 %copy-start.5 = (s32[1,2]{1,0:T(1,128)S(1)}, s32[1,2]{1,0:T(1,128)}, u32[]{:S(2)}) copy-start(s32[1,2]{1,0:T(1,128)} %param.11) | copy-start | bytes 28
  70.1 3.7 %collective-permute-start.5 = (f32[8,128]{1,0:T(8,128)S(1)}, f32[8,128]{1,0:T(8,128)S(1)}, u32[]{:S(2)}, u32[]{:S(2)}) collective-permute-start(f32[8,128]{1,0:T(8,128)S(1)} %get-tuple-element.29.mine_ref), channel_id=1, source_target_pairs={{0,1},{1,0},{2,3},{3,2},{4,5},{5,4},{6,7},{7,6},{8,9},{9,8},{10,11... | collective-permute-start | bytes 12296 | tf_op jit(solution)/shard_map/ppermute | solution.py:368
  73.8 9.0 %copy-start.3 = (bf16[1,14,2,128,128]{4,3,2,1,0:T(8,128)(2,1)S(1)}, bf16[1,14,2,128,128]{4,3,2,1,0:T(8,128)(2,1)}, u32[]{:S(2)}) copy-start(bf16[1,14,2,128,128]{4,3,2,1,0:T(8,128)(2,1)} %param.8) | copy-start | bytes 2752516
  82.7 1.2 copy-start.6
  95.4 16.6 %collective-permute-start.8 = (bf16[6,2,128,128]{3,2,1,0:T(8,128)(2,1)S(1)}, bf16[6,2,128,128]{3,2,1,0:T(8,128)(2,1)S(1)}, u32[]{:S(2)}, u32[]{:S(2)}) collective-permute-start(bf16[6,2,128,128]{3,2,1,0:T(8,128)(2,1)S(1)} %shard_map.93), channel_id=1, source_target_pairs={{2,0},{4,2},{6,4},{8,6},{10,8},{12,10},{14,12},{16,14},{18,16},{20... | collective-permute-start | bytes 1179656 | tf_op jit(solution)/shard_map/ppermute | solution.py:434
  97.3 14.7 %collective-permute-start.9 = (bf16[8,2,128,128]{3,2,1,0:T(8,128)(2,1)S(1)}, bf16[8,2,128,128]{3,2,1,0:T(8,128)(2,1)S(1)}, u32[]{:S(2)}, u32[]{:S(2)}) collective-permute-start(bf16[8,2,128,128]{3,2,1,0:T(8,128)(2,1)S(1)} %shard_map.94), channel_id=1, source_target_pairs={{2,0},{4,2},{6,4},{8,6},{10,8},{12,10},{14,12},{16,14},{18,16},{20... | collective-permute-start | bytes 1572872 | tf_op jit(solution)/shard_map/ppermute | solution.py:434
  107.0 15.6 %collective-permute-start.7 = (bf16[8,2,128,128]{3,2,1,0:T(8,128)(2,1)S(1)}, bf16[8,2,128,128]{3,2,1,0:T(8,128)(2,1)S(1)}, u32[]{:S(2)}, u32[]{:S(2)}) collective-permute-start(bf16[8,2,128,128]{3,2,1,0:T(8,128)(2,1)S(1)} %shard_map.92), channel_id=1, source_target_pairs={{0,2},{2,4},{4,6},{6,8},{8,10},{10,12},{12,14},{14,16},{16,18},{18... | collective-permute-start | bytes 1572872 | tf_op jit(solution)/shard_map/ppermute | solution.py:434
  108.9 13.7 %collective-permute-start.6 = (bf16[6,2,128,128]{3,2,1,0:T(8,128)(2,1)S(1)}, bf16[6,2,128,128]{3,2,1,0:T(8,128)(2,1)S(1)}, u32[]{:S(2)}, u32[]{:S(2)}) collective-permute-start(bf16[6,2,128,128]{3,2,1,0:T(8,128)(2,1)S(1)} %get-tuple-element.31), channel_id=1, source_target_pairs={{0,2},{2,4},{4,6},{6,8},{8,10},{10,12},{12,14},{14,16},{16,18},{18... | collective-permute-start | bytes 1179656 | tf_op jit(solution)/shard_map/ppermute | solution.py:434
where the time goes:
time: 126 us; the launch traced here: 124 us
  Pallas kernels  81.6 us (65%)
  waiting for transfers between devices  19.2 us (15%)
  starting transfers between devices  14.5 us (12%)
  local copies, waits for them, and re-layouts  5.03 us (4%)
  other arithmetic  2.72 us (2%)
    pallas_call x10, Pallas kernels, call(): pl.pallas_call(body, in_specs=specs, out_specs=jax.tree.map(lambda _: VME...  81.6 us
    ppermute x4, starting transfers between devices, sent(): lax.ppermute(value, 'seg', [(s, s + steps) for s in range(begin, end)])  10 us
    ppermute x6, waiting for transfers between devices, trade(): return lax.ppermute(value, 'blk', swap)  9.94 us
    ppermute x4, waiting for transfers between devices, sent(): lax.ppermute(value, 'seg', [(s, s + steps) for s in range(begin, end)])  9.26 us
    ppermute x6, starting transfers between devices, trade(): return lax.ppermute(value, 'blk', swap)  4.48 us
  transfers between devices with their start and end apart: 10, of which 4 were waited for; matrix products, arithmetic and copies ran while one was open for 1% of the time, Pallas kernels for 36%

commit v1 on v0

--- a/solution.py
+++ b/solution.py
@@ -16,6 +16,7 @@
 BF16 = jnp.bfloat16
 VMEM = pl.BlockSpec(memory_space=pltpu.VMEM)
 SMEM = pl.BlockSpec(memory_space=pltpu.SMEM)
+COST = pl.CostEstimate(flops=1024, bytes_accessed=1024, transcendentals=0)
 PARAMS = pltpu.CompilerParams(vmem_limit_bytes=32 * 1024 * 1024)
 
 
@@ -102,18 +103,18 @@
                             p * ROWS : (p + 1) * ROWS, j * LANES : (j + 1) * LANES
                         ]
             left = left_ref[k, dest]
-            for c in range(phys // 2):
-                cols = slice(c * 2 * LANES, (c + 1) * 2 * LANES)
-                part_ref[i, :, cols] = dot(left, mixed_ref[i, :, cols]).astype(BF16)
+            part = dot(left, mixed_ref[i]).astype(BF16)
+            for p in range(phys):
+                part_ref[p * rows : (p + 1) * rows, i * LANES : (i + 1) * LANES] = part[
+                    :, p * LANES : (p + 1) * LANES
+                ]
             right = right_t_ref[k, dest]
             if i == 1:
                 right = jnp.where(live_list[2 * s + 1] > 0, right, jnp.zeros_like(right))
             weights.append(right)
-        both = jnp.concatenate(weights, axis=0)
+        image = dot(part_ref[...], jnp.concatenate(weights, axis=0))
         for p in range(phys):
-            cols = slice(p * LANES, (p + 1) * LANES)
-            pair = jnp.concatenate([part_ref[0, :, cols], part_ref[1, :, cols]], axis=1)
-            acc_ref[dest, :, cols] += dot(pair, both)
+            acc_ref[dest, :, p * LANES : (p + 1) * LANES] += image[p * rows : (p + 1) * rows]
         return carry
 
     lax.fori_loop(0, steps, step, 0)
@@ -156,7 +157,7 @@
 
     def turn(n, carry):
         k, b = n // dests, lax.rem(n, dests)
-        right_t_ref[k, b] = right_ref[k, b].astype(F32).T.astype(BF16)
+        right_t_ref[k, b] = right_ref[k, b].T
         return carry
 
     lax.fori_loop(0, chan * dests, turn, 0)
@@ -311,32 +312,35 @@
     def turn(n, carry):
         b, p = n // times, lax.rem(n, times)
         cols = pl.ds(pl.multiple_of(p * LANES, LANES), LANES)
-        turned_ref[b, :, cols] = state_ref[b, :, cols].astype(F32).T.astype(BF16)
+        turned_ref[b, :, cols] = state_ref[b, :, cols].T
         return carry
 
     lax.fori_loop(0, blocks * times, turn, 0)
 
 
-def environments(first, count, scale, env_ref, inner_ref, outer_ref, out_ref, mid_ref):
-    dests = env_ref.shape[1]
-    phys = inner_ref.shape[2] // LANES
+def environments(first, count, scale, env_ref, outer_ref, inner_ref, out_ref, mid_ref):
+    dests, rows, width = outer_ref.shape
+    phys = width // LANES
 
     def step(n, carry):
         pair, b = n // dests, lax.rem(n, dests)
         k = first + 2 * pair
-        env = jnp.concatenate([env_ref[k, b], env_ref[k + 1, b]], axis=0)
-        for c in range(phys // 2):
-            cols = slice(c * 2 * LANES, (c + 1) * 2 * LANES)
-            mid = dot(env, inner_ref[b, :, cols]).astype(BF16)
-            for h in range(2):
-                p = 2 * c + h
-                for i in range(2):
-                    mid_ref[p * LANES : (p + 1) * LANES, i * LANES : (i + 1) * LANES] = mid[
-                        i * LANES : (i + 1) * LANES, h * LANES : (h + 1) * LANES
-                    ]
-        out = (dot(outer_ref[b], mid_ref[...]) * scale).astype(BF16)
-        out_ref[2 * pair, b] = out[:, :LANES]
-        out_ref[2 * pair + 1, b] = out[:, LANES:]
+        env = jnp.concatenate([env_ref[k, b], env_ref[k + 1, b]], axis=1)
+        tall = jnp.concatenate(
+            [outer_ref[b, :, p * LANES : (p + 1) * LANES] for p in range(phys)], axis=0
+        )
+        mid = dot(tall, env).astype(BF16)
+        for p in range(phys):
+            for i in range(2):
+                mid_ref[i * rows : (i + 1) * rows, p * LANES : (p + 1) * LANES] = mid[
+                    p * rows : (p + 1) * rows, i * LANES : (i + 1) * LANES
+                ]
+        last = jnp.concatenate(
+            [inner_ref[b, :, p * LANES : (p + 1) * LANES] for p in range(phys)], axis=0
+        )
+        out = (dot(mid_ref[...], last) * scale).astype(BF16)
+        out_ref[2 * pair, b] = out[:rows]
+        out_ref[2 * pair + 1, b] = out[rows:]
         return carry
 
     lax.fori_loop(0, (count // 2) * dests, step, 0)
@@ -345,11 +349,33 @@
 def normalize_and_left(
     first, count, scale, cells,
     kept_ref, first_ref, mine_ref, theirs_ref, env_ref,
-    state_ref, turned_ref, out_ref,
-    mid_ref,
+    new_ref, state_ref, turned_ref, out_ref,
+    mid_ref, sem,
 ):
     normalize(cells, kept_ref, first_ref, mine_ref, theirs_ref, state_ref, turned_ref)
-    environments(first, count, scale, env_ref, state_ref, turned_ref, out_ref, mid_ref)
+    copy = pltpu.make_async_copy(state_ref, new_ref, sem)
+    copy.start()
+    environments(first, count, scale, env_ref, turned_ref, state_ref, out_ref, mid_ref)
+    copy.wait()
+
+
+def widen(places, *refs):
+    pieces, outs, wides, sems = refs[:4], refs[4:6], refs[6:8], refs[8]
+    copies = []
+    for n, (piece, (side, begin)) in enumerate(zip(pieces, places)):
+        count = piece.shape[0]
+
+        def one(k, carry):
+            wides[side][begin + k] = piece[k].astype(F32)
+            return carry
+
+        lax.fori_loop(0, count, one, 0)
+        span = pl.ds(begin, count)
+        copy = pltpu.make_async_copy(wides[side].at[span], outs[side].at[span], sems.at[n])
+        copy.start()
+        copies.append(copy)
+    for copy in copies:
+        copy.wait()
 
 
 def shards(state, left_env, right_env, site_ops, sector_map, ranks):
@@ -375,10 +401,11 @@
     wave_b16 = shape(wave, BF16)
     sums_kind = shape((8, LANES), F32)
     lists = [pltpu.SMEM((chan * dests + 2 * dests + 1,), jnp.int32)] * 4
-    pair_scratch = [pltpu.VMEM((2, rows, width), BF16)] * 2 + lists
-    one_apply = 2 * chan * dests * rows * width * (ROWS * phys + 2 * rows)
-
-    def call(body, specs, outs, scratch, share, *args):
+    pair_scratch = [
+        pltpu.VMEM((2, rows, width), BF16), pltpu.VMEM((phys * rows, 2 * LANES), BF16)
+    ] + lists
+
+    def call(body, specs, outs, scratch, *args):
         return pl.pallas_call(
             body,
             in_specs=specs,
@@ -386,47 +413,44 @@
             out_shape=outs,
             scratch_shapes=scratch,
             compiler_params=PARAMS,
-            cost_estimate=pl.CostEstimate(
-                flops=int(one_apply * share), bytes_accessed=8 * 1024 * 1024, transcendentals=0
-            ),
+            cost_estimate=COST,
         )(*args)
 
     other = [trade(x[b : b + 1]) for b in range(dests)]
     kron, right_t, image_local, sums_local = call(
         first_local, [SMEM] + [VMEM] * 4,
         (shape((chan, phys * ROWS, phys * ROWS), BF16), shape(right.shape, BF16), wave_f32, sums_kind),
-        pair_scratch, 0.7, rel, ops, x, left, right,
+        pair_scratch, rel, ops, x, left, right,
     )
     image_remote = call(
-        first_remote, [SMEM] + [VMEM] * 4, wave_f32, pair_scratch, 0.25,
+        first_remote, [SMEM] + [VMEM] * 4, wave_f32, pair_scratch,
         rel, kron, other[0], left, right_t,
     )
     image_remote, guess, mine = call(
-        first_finish, [SMEM] + [VMEM] * 8, (wave_f32, wave_b16, sums_kind), pair_scratch, 0.3,
+        first_finish, [SMEM] + [VMEM] * 8, (wave_f32, wave_b16, sums_kind), pair_scratch,
         rel, kron, other[1], left, right_t, image_remote, x, image_local, sums_local,
     )
     theirs = trade(mine)
     other = [trade(guess[b : b + 1]) for b in range(dests)]
     acc = call(
-        second_local, [SMEM] + [VMEM] * 4, wave_f32, pair_scratch, 0.5,
+        second_local, [SMEM] + [VMEM] * 4, wave_f32, pair_scratch,
         rel, kron, guess, left, right_t,
     )
     acc, first = call(
-        second_remote, [SMEM] + [VMEM] * 10, (wave_f32, wave_b16), pair_scratch, 0.25,
+        second_remote, [SMEM] + [VMEM] * 10, (wave_f32, wave_b16), pair_scratch,
         rel, kron, other[0], left, right_t, acc, x, image_local, image_remote, mine, theirs,
     )
     kept, kept_first, sums_mine = call(
         second_finish, [SMEM, SMEM] + [VMEM] * 8, (wave_f32, wave_b16, sums_kind),
-        [pltpu.VMEM(wave, F32)] + pair_scratch, 0.3,
+        [pltpu.VMEM(wave, F32)] + pair_scratch,
         rel, ranks[0], kron, other[1], left, right_t, acc, first, mine, theirs,
     )
     sums_theirs = trade(sums_mine)
 
     env_scale = 1.0 / math.sqrt(phys * rows)
     cells = float(total_blocks * rows * width)
-    half = chan // 4 * 2
-    cuts = [(0, half), (half, chan - half)]
-    mid = [pltpu.VMEM((width, 2 * LANES), BF16)]
+    early, later = 10, 8
+    mid = [pltpu.VMEM((2 * rows, width), BF16)]
 
     def sent(value, steps):
         count = lax.axis_size("seg")
@@ -436,27 +460,37 @@
     def env_kind(count):
         return shape((count,) + left.shape[1:], BF16)
 
-    lefts, rights = [], []
-    for n, (begin, count) in enumerate(cuts):
-        if n == 0:
-            new_state, turned, piece = call(
-                functools.partial(normalize_and_left, begin, count, env_scale, cells),
-                [VMEM] * 5, (wave_b16, wave_b16, env_kind(count)), mid, 0.3,
-                kept, kept_first, sums_mine, sums_theirs, left,
-            )
-        else:
-            piece = call(
-                functools.partial(environments, begin, count, env_scale),
-                [VMEM] * 3, env_kind(count), mid, 0.3, left, new_state, turned,
-            )
-        lefts.append(sent(piece, 1))
-        piece = call(
+    def env_call(begin, count, env, outer, inner):
+        return call(
             functools.partial(environments, begin, count, env_scale),
-            [VMEM] * 3, env_kind(count), mid, 0.3, right, turned, new_state,
+            [VMEM] * 3, env_kind(count), mid, env, outer, inner,
         )
-        rights.append(sent(piece, -1))
-    received_left = jnp.concatenate(lefts, axis=0).astype(F32)
-    received_right = jnp.concatenate(rights, axis=0).astype(F32)
+
+    new_state, state_kept, turned, piece = pl.pallas_call(
+        functools.partial(normalize_and_left, 0, early, env_scale, cells),
+        in_specs=[VMEM] * 5,
+        out_specs=(pl.BlockSpec(memory_space=pltpu.HBM), VMEM, VMEM, VMEM),
+        out_shape=(wave_b16, wave_b16, wave_b16, env_kind(early)),
+        scratch_shapes=mid + [pltpu.SemaphoreType.DMA],
+        compiler_params=PARAMS,
+        cost_estimate=COST,
+    )(kept, kept_first, sums_mine, sums_theirs, left)
+    lefts = [sent(piece, 1)]
+    rights = [
+        sent(env_call(0, later, right, state_kept, turned), -1),
+        sent(env_call(later, chan - later, right, state_kept, turned), -1),
+    ]
+    lefts.append(sent(env_call(early, chan - early, left, turned, state_kept), 1))
+    env_f32 = shape(left.shape, F32)
+    received_left, received_right = pl.pallas_call(
+        functools.partial(widen, ((0, 0), (1, 0), (1, later), (0, early))),
+        in_specs=[VMEM] * 4,
+        out_specs=(pl.BlockSpec(memory_space=pltpu.HBM),) * 2,
+        out_shape=(env_f32, env_f32),
+        scratch_shapes=[pltpu.VMEM(left.shape, F32)] * 2 + [pltpu.SemaphoreType.DMA((4,))],
+        compiler_params=PARAMS,
+        cost_estimate=COST,
+    )(lefts[0], rights[0], rights[1], lefts[1])
     return (new_state[None], received_left[None], received_right[None])
 
 

time: 126 us -> 129 us (1.024)
  the two profiles are of different devices: /device:TPU:16 before, /device:TPU:1 now
where the time goes in v1:
time: 129 us; the launch traced here: 127 us
  Pallas kernels  86.9 us (67%)
  starting transfers between devices  19.6 us (15%)
  waiting for transfers between devices  15.7 us (12%)
  local copies, waits for them, and re-layouts  3.81 us (3%)
    pallas_call x9, Pallas kernels, call(): pl.pallas_call(body, in_specs=specs, out_specs=jax.tree.map(lambda _: VME...  72.4 us
    ppermute x4, starting transfers between devices, sent(): lax.ppermute(value, 'seg', [(s, s + steps) for s in range(begin, end)])  15.7 us
    pallas_call x1, Pallas kernels, shards(): pl.pallas_call(functools.partial(normalize_and_left, 0, early, env_scale,...  12.5 us
    ppermute x6, waiting for transfers between devices, trade(): return lax.ppermute(value, 'blk', swap)  12.4 us
    ppermute x6, starting transfers between devices, trade(): return lax.ppermute(value, 'blk', swap)  3.87 us
    ppermute x4, waiting for transfers between devices, sent(): lax.ppermute(value, 'seg', [(s, s + steps) for s in range(begin, end)])  3.3 us
  transfers between devices with their start and end apart: 10, of which 3 were waited for; matrix products, arithmetic and copies ran while one was open for 0% of the time, Pallas kernels for 46%

profile of v1, /device:TPU:1, one launch (start us, length us, event | category | flops | bytes accessed | tf_op | source)
XLA Modules:
  0.0 126.9 jit_solution(2741097823701963881)
XLA Ops:
  0.6 0.0 copy-start.1
  0.6 0.0 copy-start.6
  0.7 0.0 copy-start.4
  0.7 0.0 copy-start
  0.7 2.4 %slice_bitcast_fusion = (bf16[1,128,2048]{2,1,0:T(8,128)(2,1)}, bf16[1,128,2048]{2,1,0:T(8,128)(2,1)}) fusion(bf16[1,2,128,2048]{3,2,1,0:T(8,128)(2,1)} %param.6), kind=kLoop, calls=%fused_computation | loop fusion | bytes 2097152 | tf_op jit(solution)/shard_map/slice | solution.py:419
  3.1 2.0 %collective-permute-start.1 = (bf16[1,128,2048]{2,1,0:T(8,128)(2,1)}, bf16[1,128,2048]{2,1,0:T(8,128)(2,1)S(1)}, u32[]{:S(2)}, u32[]{:S(2)}) collective-permute-start(bf16[1,128,2048]{2,1,0:T(8,128)(2,1)} %get-tuple-element.41), channel_id=1, source_target_pairs={{0,1},{1,0},{2,3},{3,2},{4,5},{5,4},{6,7},{7,6},{8,9},{9,8},{10,11... | collective-permute-start | bytes 1572872 | tf_op jit(solution)/shard_map/ppermute | solution.py:394
  5.1 0.0 collective-permute-start
  5.2 0.0 copy-done.6
  5.2 0.1 copy.9
  5.3 0.0 copy-done.1
  5.3 0.0 copy-done.4
  5.3 0.0 copy-done
  5.3 0.0 copy-start.2
  5.3 1.2 copy-done.2
  6.5 19.1 %shard_map.85 = (bf16[14,256,256]{2,1,0:T(8,128)(2,1)S(1)}, bf16[14,2,128,128]{3,2,1,0:T(8,128)(2,1)S(1)}, f32[2,128,2048]{2,1,0:T(8,128)S(1)}, f32[8,128]{1,0:T(8,128)S(1)}) custom-call(s32[14,2]{1,0:T(8,128)S(1)} %negate_select_fusion.rel_ref, bf16[14,16,16]{2,1,0:T(8,128)(2,1)S(1)} %bitcast.28, bf16[2,128,2048]{2,1,0:T(8,128)(2,1)S(1)} %bitcast.22, ...), custom_call_target="tpu_custom_call" | custom-call | flops 1024 | bytes 1024 | tf_op jit(solution)/shard_map/pallas_call | solution.py:409
  25.6 0.0 collective-permute-done.1.other_ref
  25.6 4.6 %shard_map.86.before_ref = f32[2,128,2048]{2,1,0:T(8,128)S(1)} custom-call(s32[14,2]{1,0:T(8,128)S(1)} %negate_select_fusion.rel_ref, bf16[14,256,256]{2,1,0:T(8,128)(2,1)S(1)} %get-tuple-element.21.kron_ref, bf16[1,128,2048]{2,1,0:T(8,128)(2,1)S(1)} %collective-permute-done.1.other_ref, bf16[14,2,128,128]{3,2,1,0:T(8,128)(2,1)S(1)} %bitcast.15, ...), custom_call_target="tpu_custom_call" | custom-call | flops 1024 | bytes 1024 | tf_op jit(solution)/shard_map/pallas_call | solution.py:409
  30.1 0.0 collective-permute-done.other_ref
  30.2 6.6 %shard_map.87 = (f32[2,128,2048]{2,1,0:T(8,128)S(1)}, bf16[2,128,2048]{2,1,0:T(8,128)(2,1)S(1)}, f32[8,128]{1,0:T(8,128)S(1)}) custom-call(s32[14,2]{1,0:T(8,128)S(1)} %negate_select_fusion.rel_ref, bf16[14,256,256]{2,1,0:T(8,128)(2,1)S(1)} %get-tuple-element.21.kron_ref, bf16[1,128,2048]{2,1,0:T(8,128)(2,1)S(1)} %collective-permute-done.other_ref, ...), custom_call_target="tpu_custom_call" | custom-call | flops 1024 | bytes 1024 | tf_op jit(solution)/shard_map/pallas_call | solution.py:409
  36.8 0.1 fusion.1
  36.9 0.3 collective-permute-start.3
  37.2 1.3 %collective-permute-start.2 = (bf16[1,128,2048]{2,1,0:T(8,128)(2,1)S(1)}, bf16[1,128,2048]{2,1,0:T(8,128)(2,1)S(1)}, u32[]{:S(2)}, u32[]{:S(2)}) collective-permute-start(bf16[1,128,2048]{2,1,0:T(8,128)(2,1)S(1)} %get-tuple-element.40), channel_id=1, source_target_pairs={{0,1},{1,0},{2,3},{3,2},{4,5},{5,4},{6,7},{7,6},{8,9},{9,8},{10,11... | collective-permute-start | bytes 1572872 | tf_op jit(solution)/shard_map/ppermute | solution.py:394
  38.4 0.2 collective-permute-start.4
  38.6 12.2 %shard_map.88.before_ref = f32[2,128,2048]{2,1,0:T(8,128)S(1)} custom-call(s32[14,2]{1,0:T(8,128)S(1)} %negate_select_fusion.rel_ref, bf16[14,256,256]{2,1,0:T(8,128)(2,1)S(1)} %get-tuple-element.21.kron_ref, bf16[2,128,2048]{2,1,0:T(8,128)(2,1)S(1)} %get-tuple-element.25.guess_ref, bf16[14,2,128,128]{3,2,1,0:T(8,128)(2,1)S(1)} %bitcast.17, ...), custom_call_target="tpu_custom_call" | custom-call | flops 1024 | bytes 1024 | tf_op jit(solution)/shard_map/pallas_call | solution.py:409
  50.8 10.0 %collective-permute-done.4.theirs_ref = f32[8,128]{1,0:T(8,128)S(1)} collective-permute-done((f32[8,128]{1,0:T(8,128)S(1)}, f32[8,128]{1,0:T(8,128)S(1)}, u32[]{:S(2)}, u32[]{:S(2)}) %collective-permute-start.4) | collective-permute-done | bytes 4128 | tf_op jit(solution)/shard_map/ppermute | solution.py:394
  60.8 0.0 collective-permute-done.3.other_ref
  60.8 0.0 copy-start.5
  60.8 5.4 %shard_map.89 = (f32[2,128,2048]{2,1,0:T(8,128)S(1)}, bf16[2,128,2048]{2,1,0:T(8,128)(2,1)S(1)}) custom-call(s32[14,2]{1,0:T(8,128)S(1)} %negate_select_fusion.rel_ref, bf16[14,256,256]{2,1,0:T(8,128)(2,1)S(1)} %get-tuple-element.21.kron_ref, bf16[1,128,2048]{2,1,0:T(8,128)(2,1)S(1)} %collective-permute-done.3.other_ref, ...), custom_call_target="tpu_custom_call" | custom-call | flops 1024 | bytes 1024 | tf_op jit(solution)/shard_map/pallas_call | solution.py:409
  66.1 0.0 collective-permute-done.2.other_ref
  66.2 0.0 copy-done.5
  66.2 7.3 %shard_map.90 = (f32[2,128,2048]{2,1,0:T(8,128)S(1)}, bf16[2,128,2048]{2,1,0:T(8,128)(2,1)S(1)}, f32[8,128]{1,0:T(8,128)S(1)}) custom-call(s32[14,2]{1,0:T(8,128)S(1)} %negate_select_fusion.rel_ref, s32[2]{0:T(128)S(1)} %bitcast.29, bf16[14,256,256]{2,1,0:T(8,128)(2,1)S(1)} %get-tuple-element.21.kron_ref, ...), custom_call_target="tpu_custom_call" | custom-call | flops 1024 | bytes 1024 | tf_op jit(solution)/shard_map/pallas_call | solution.py:409
  73.5 0.0 copy-start.3
  73.5 0.1 collective-permute-start.5
  73.6 2.4 %collective-permute-done.5.theirs_ref = f32[8,128]{1,0:T(8,128)S(1)} collective-permute-done((f32[8,128]{1,0:T(8,128)S(1)}, f32[8,128]{1,0:T(8,128)S(1)}, u32[]{:S(2)}, u32[]{:S(2)}) %collective-permute-start.5) | collective-permute-done | bytes 4128 | tf_op jit(solution)/shard_map/ppermute | solution.py:394
  76.0 12.5 %shard_map.91 = (bf16[2,128,2048]{2,1,0:T(8,128)(2,1)}, bf16[2,128,2048]{2,1,0:T(8,128)(2,1)S(1)}, bf16[2,128,2048]{2,1,0:T(8,128)(2,1)S(1)}, bf16[10,2,128,128]{3,2,1,0:T(8,128)(2,1)S(1)}) custom-call(f32[2,128,2048]{2,1,0:T(8,128)S(1)} %get-tuple-element.30.kept_ref, bf16[2,128,2048]{2,1,0:T(8,128)(2,1)S(1)} %get-tuple-element.31.first_ref, ...), custom_call_target="tpu_custom_call" | custom-call | flops 1024 | bytes 1024 | tf_op jit(solution)/shard_map/pallas_call | solution.py:469
  88.6 8.2 %collective-permute-start.6 = (bf16[10,2,128,128]{3,2,1,0:T(8,128)(2,1)S(1)}, bf16[10,2,128,128]{3,2,1,0:T(8,128)(2,1)S(1)}, u32[]{:S(2)}, u32[]{:S(2)}) collective-permute-start(bf16[10,2,128,128]{3,2,1,0:T(8,128)(2,1)S(1)} %get-tuple-element.34), channel_id=1, source_target_pairs={{0,2},{2,4},{4,6},{6,8},{8,10},{10,12},{12,14},{14,16},{16,18},{18... | collective-permute-start | bytes 1966088 | tf_op jit(solution)/shard_map/ppermute | solution.py:458
  96.8 0.0 copy-done.3
  96.8 7.7 %shard_map.92 = bf16[8,2,128,128]{3,2,1,0:T(8,128)(2,1)S(1)} custom-call(bf16[14,2,128,128]{3,2,1,0:T(8,128)(2,1)S(1)} %bitcast.26, bf16[2,128,2048]{2,1,0:T(8,128)(2,1)S(1)} %get-tuple-element.35.outer_ref.inner_ref, bf16[2,128,2048]{2,1,0:T(8,128)(2,1)S(1)} %get-tuple-element.36.inner_ref.outer_ref), custom_call_target="tpu_custom_call" | custom-call | flops 1024 | bytes 1024 | tf_op jit(solution)/shard_map/pallas_call | solution.py:409
  104.5 1.9 %collective-permute-start.7 = (bf16[8,2,128,128]{3,2,1,0:T(8,128)(2,1)S(1)}, bf16[8,2,128,128]{3,2,1,0:T(8,128)(2,1)S(1)}, u32[]{:S(2)}, u32[]{:S(2)}) collective-permute-start(bf16[8,2,128,128]{3,2,1,0:T(8,128)(2,1)S(1)} %shard_map.92), channel_id=1, source_target_pairs={{2,0},{4,2},{6,4},{8,6},{10,8},{12,10},{14,12},{16,14},{18,16},{20... | collective-permute-start | bytes 1572872 | tf_op jit(solution)/shard_map/ppermute | solution.py:458
  106.4 5.8 %shard_map.93 = bf16[6,2,128,128]{3,2,1,0:T(8,128)(2,1)S(1)} custom-call(bf16[14,2,128,128]{3,2,1,0:T(8,128)(2,1)S(1)} %bitcast.27, bf16[2,128,2048]{2,1,0:T(8,128)(2,1)S(1)} %get-tuple-element.35.outer_ref.inner_ref, bf16[2,128,2048]{2,1,0:T(8,128)(2,1)S(1)} %get-tuple-element.36.inner_ref.outer_ref), custom_call_target="tpu_custom_call" | custom-call | flops 1024 | bytes 1024 | tf_op jit(solution)/shard_map/pallas_call | solution.py:409
  112.2 1.9 %collective-permute-start.8 = (bf16[6,2,128,128]{3,2,1,0:T(8,128)(2,1)S(1)}, bf16[6,2,128,128]{3,2,1,0:T(8,128)(2,1)S(1)}, u32[]{:S(2)}, u32[]{:S(2)}) collective-permute-start(bf16[6,2,128,128]{3,2,1,0:T(8,128)(2,1)S(1)} %shard_map.93), channel_id=1, source_target_pairs={{2,0},{4,2},{6,4},{8,6},{10,8},{12,10},{14,12},{16,14},{18,16},{20... | collective-permute-start | bytes 1179656 | tf_op jit(solution)/shard_map/ppermute | solution.py:458
  114.1 3.8 %shard_map.94 = bf16[4,2,128,128]{3,2,1,0:T(8,128)(2,1)S(1)} custom-call(bf16[14,2,128,128]{3,2,1,0:T(8,128)(2,1)S(1)} %bitcast.21, bf16[2,128,2048]{2,1,0:T(8,128)(2,1)S(1)} %get-tuple-element.36.inner_ref.outer_ref, bf16[2,128,2048]{2,1,0:T(8,128)(2,1)S(1)} %get-tuple-element.35.outer_ref.inner_ref), custom_call_target="tpu_custom_call" | custom-call | flops 1024 | bytes 1024 | tf_op jit(solution)/shard_map/pallas_call | solution.py:409
  118.0 3.6 %collective-permute-start.9 = (bf16[4,2,128,128]{3,2,1,0:T(8,128)(2,1)S(1)}, bf16[4,2,128,128]{3,2,1,0:T(8,128)(2,1)S(1)}, u32[]{:S(2)}, u32[]{:S(2)}) collective-permute-start(bf16[4,2,128,128]{3,2,1,0:T(8,128)(2,1)S(1)} %shard_map.94), channel_id=1, source_target_pairs={{0,2},{2,4},{4,6},{6,8},{8,10},{10,12},{12,14},{14,16},{16,18},{18... | collective-permute-start | bytes 786440 | tf_op jit(solution)/shard_map/ppermute | solution.py:458
  121.6 3.3 %collective-permute-done.9.refs_3_ = bf16[4,2,128,128]{3,2,1,0:T(8,128)(2,1)S(1)} collective-permute-done((bf16[4,2,128,128]{3,2,1,0:T(8,128)(2,1)S(1)}, bf16[4,2,128,128]{3,2,1,0:T(8,128)(2,1)S(1)}, u32[]{:S(2)}, u32[]{:S(2)}) %collective-permute-start.9) | collective-permute-done | bytes 262176 | tf_op jit(solution)/shard_map/ppermute | solution.py:458
  124.9 0.0 collective-permute-done.8.refs_2_
  124.9 0.0 collective-permute-done.7.refs_1_
  124.9 0.0 collective-permute-done.6.refs_0_
  124.9 2.0 %shard_map.95 = (f32[14,2,128,128]{3,2,1,0:T(8,128)}, f32[14,2,128,128]{3,2,1,0:T(8,128)}) custom-call(bf16[10,2,128,128]{3,2,1,0:T(8,128)(2,1)S(1)} %collective-permute-done.6.refs_0_, bf16[8,2,128,128]{3,2,1,0:T(8,128)(2,1)S(1)} %collective-permute-done.7.refs_1_, bf16[6,2,128,128]{3,2,1,0:T(8,128)(2,1)S(1)} %collective-permute-done.8.refs_2_, ...), custom_call_target="tpu_custom_call" | custom-call | flops 1024 | bytes 1024 | tf_op jit(solution)/shard_map/pallas_call | solution.py:485
  (2 shorter events, 0.0 us)
Async XLA Ops:
  0.6 4.6 %copy-start.1 = (bf16[1,2,128,2048]{3,2,1,0:T(8,128)(2,1)S(1)}, bf16[1,2,128,2048]{3,2,1,0:T(8,128)(2,1)}, u32[]{:S(2)}) copy-start(bf16[1,2,128,2048]{3,2,1,0:T(8,128)(2,1)} %param.6) | copy-start | bytes 3145732
  0.6 4.5 %copy-start.6 = (s32[1,14,4]{1,2,0:T(4,128)S(1)}, s32[1,14,4]{1,2,0:T(4,128)}, u32[]{:S(2)}) copy-start(s32[1,14,4]{1,2,0:T(4,128)} %param.10) | copy-start | bytes 676
  0.7 4.6 %copy-start.4 = (bf16[1,14,16,16]{3,2,1,0:T(8,128)(2,1)S(1)}, bf16[1,14,16,16]{3,2,1,0:T(8,128)(2,1)}, u32[]{:S(2)}) copy-start(bf16[1,14,16,16]{3,2,1,0:T(8,128)(2,1)} %param.9) | copy-start | bytes 21508
  0.7 4.6 %copy-start = (bf16[1,14,2,128,128]{4,3,2,1,0:T(8,128)(2,1)S(1)}, bf16[1,14,2,128,128]{4,3,2,1,0:T(8,128)(2,1)}, u32[]{:S(2)}) copy-start(bf16[1,14,2,128,128]{4,3,2,1,0:T(8,128)(2,1)} %param.7) | copy-start | bytes 2752516
  3.1 22.5 %collective-permute-start.1 = (bf16[1,128,2048]{2,1,0:T(8,128)(2,1)}, bf16[1,128,2048]{2,1,0:T(8,128)(2,1)S(1)}, u32[]{:S(2)}, u32[]{:S(2)}) collective-permute-start(bf16[1,128,2048]{2,1,0:T(8,128)(2,1)} %get-tuple-element.41), channel_id=1, source_target_pairs={{0,1},{1,0},{2,3},{3,2},{4,5},{5,4},{6,7},{7,6},{8,9},{9,8},{10,11... | collective-permute-start | bytes 1572872 | tf_op jit(solution)/shard_map/ppermute | solution.py:394
  5.1 25.0 %collective-permute-start = (bf16[1,128,2048]{2,1,0:T(8,128)(2,1)}, bf16[1,128,2048]{2,1,0:T(8,128)(2,1)S(1)}, u32[]{:S(2)}, u32[]{:S(2)}) collective-permute-start(bf16[1,128,2048]{2,1,0:T(8,128)(2,1)} %get-tuple-element.42), channel_id=1, source_target_pairs={{0,1},{1,0},{2,3},{3,2},{4,5},{5,4},{6,7},{7,6},{8,9},{9,8},{10,11... | collective-permute-start | bytes 1572872 | tf_op jit(solution)/shard_map/ppermute | solution.py:394
  5.3 1.2 copy-start.2
  36.9 23.8 %collective-permute-start.3 = (bf16[1,128,2048]{2,1,0:T(8,128)(2,1)S(1)}, bf16[1,128,2048]{2,1,0:T(8,128)(2,1)S(1)}, u32[]{:S(2)}, u32[]{:S(2)}) collective-permute-start(bf16[1,128,2048]{2,1,0:T(8,128)(2,1)S(1)} %get-tuple-element.39), channel_id=1, source_target_pairs={{0,1},{1,0},{2,3},{3,2},{4,5},{5,4},{6,7},{7,6},{8,9},{9,8},{10,11... | collective-permute-start | bytes 1572872 | tf_op jit(solution)/shard_map/ppermute | solution.py:394
  37.2 29.0 %collective-permute-start.2 = (bf16[1,128,2048]{2,1,0:T(8,128)(2,1)S(1)}, bf16[1,128,2048]{2,1,0:T(8,128)(2,1)S(1)}, u32[]{:S(2)}, u32[]{:S(2)}) collective-permute-start(bf16[1,128,2048]{2,1,0:T(8,128)(2,1)S(1)} %get-tuple-element.40), channel_id=1, source_target_pairs={{0,1},{1,0},{2,3},{3,2},{4,5},{5,4},{6,7},{7,6},{8,9},{9,8},{10,11... | collective-permute-start | bytes 1572872 | tf_op jit(solution)/shard_map/ppermute | solution.py:394
  38.4 22.3 %collective-permute-start.4 = (f32[8,128]{1,0:T(8,128)S(1)}, f32[8,128]{1,0:T(8,128)S(1)}, u32[]{:S(2)}, u32[]{:S(2)}) collective-permute-start(f32[8,128]{1,0:T(8,128)S(1)} %get-tuple-element.27.mine_ref), channel_id=1, source_target_pairs={{0,1},{1,0},{2,3},{3,2},{4,5},{5,4},{6,7},{7,6},{8,9},{9,8},{10,11... | collective-permute-start | bytes 12296 | tf_op jit(solution)/shard_map/ppermute | solution.py:394
  60.8 5.4 %copy-start.5 = (s32[1,2]{1,0:T(1,128)S(1)}, s32[1,2]{1,0:T(1,128)}, u32[]{:S(2)}) copy-start(s32[1,2]{1,0:T(1,128)} %param.11) | copy-start | bytes 28
  73.5 23.3 %copy-start.3 = (bf16[1,14,2,128,128]{4,3,2,1,0:T(8,128)(2,1)S(1)}, bf16[1,14,2,128,128]{4,3,2,1,0:T(8,128)(2,1)}, u32[]{:S(2)}) copy-start(bf16[1,14,2,128,128]{4,3,2,1,0:T(8,128)(2,1)} %param.8) | copy-start | bytes 2752516
  73.5 2.5 %collective-permute-start.5 = (f32[8,128]{1,0:T(8,128)S(1)}, f32[8,128]{1,0:T(8,128)S(1)}, u32[]{:S(2)}, u32[]{:S(2)}) collective-permute-start(f32[8,128]{1,0:T(8,128)S(1)} %get-tuple-element.32.mine_ref), channel_id=1, source_target_pairs={{0,1},{1,0},{2,3},{3,2},{4,5},{5,4},{6,7},{7,6},{8,9},{9,8},{10,11... | collective-permute-start | bytes 12296 | tf_op jit(solution)/shard_map/ppermute | solution.py:394
  88.6 36.4 %collective-permute-start.6 = (bf16[10,2,128,128]{3,2,1,0:T(8,128)(2,1)S(1)}, bf16[10,2,128,128]{3,2,1,0:T(8,128)(2,1)S(1)}, u32[]{:S(2)}, u32[]{:S(2)}) collective-permute-start(bf16[10,2,128,128]{3,2,1,0:T(8,128)(2,1)S(1)} %get-tuple-element.34), channel_id=1, source_target_pairs={{0,2},{2,4},{4,6},{6,8},{8,10},{10,12},{12,14},{14,16},{16,18},{18... | collective-permute-start | bytes 1966088 | tf_op jit(solution)/shard_map/ppermute | solution.py:458
  104.5 20.4 %collective-permute-start.7 = (bf16[8,2,128,128]{3,2,1,0:T(8,128)(2,1)S(1)}, bf16[8,2,128,128]{3,2,1,0:T(8,128)(2,1)S(1)}, u32[]{:S(2)}, u32[]{:S(2)}) collective-permute-start(bf16[8,2,128,128]{3,2,1,0:T(8,128)(2,1)S(1)} %shard_map.92), channel_id=1, source_target_pairs={{2,0},{4,2},{6,4},{8,6},{10,8},{12,10},{14,12},{16,14},{18,16},{20... | collective-permute-start | bytes 1572872 | tf_op jit(solution)/shard_map/ppermute | solution.py:458
  112.2 12.7 %collective-permute-start.8 = (bf16[6,2,128,128]{3,2,1,0:T(8,128)(2,1)S(1)}, bf16[6,2,128,128]{3,2,1,0:T(8,128)(2,1)S(1)}, u32[]{:S(2)}, u32[]{:S(2)}) collective-permute-start(bf16[6,2,128,128]{3,2,1,0:T(8,128)(2,1)S(1)} %shard_map.93), channel_id=1, source_target_pairs={{2,0},{4,2},{6,4},{8,6},{10,8},{12,10},{14,12},{16,14},{18,16},{20... | collective-permute-start | bytes 1179656 | tf_op jit(solution)/shard_map/ppermute | solution.py:458
  118.0 6.9 %collective-permute-start.9 = (bf16[4,2,128,128]{3,2,1,0:T(8,128)(2,1)S(1)}, bf16[4,2,128,128]{3,2,1,0:T(8,128)(2,1)S(1)}, u32[]{:S(2)}, u32[]{:S(2)}) collective-permute-start(bf16[4,2,128,128]{3,2,1,0:T(8,128)(2,1)S(1)} %shard_map.94), channel_id=1, source_target_pairs={{0,2},{2,4},{4,6},{6,8},{8,10},{10,12},{12,14},{14,16},{16,18},{18... | collective-permute-start | bytes 786440 | tf_op jit(solution)/shard_map/ppermute | solution.py:458

commit v2 on v1

--- a/solution.py
+++ b/solution.py
@@ -12,9 +12,11 @@
 EPSILON = 1e-06
 LANES = 128
 ROWS = 16
+CHUNK = 32
 F32 = jnp.float32
 BF16 = jnp.bfloat16
 VMEM = pl.BlockSpec(memory_space=pltpu.VMEM)
+HBM = pl.BlockSpec(memory_space=pltpu.HBM)
 SMEM = pl.BlockSpec(memory_space=pltpu.SMEM)
 COST = pl.CostEstimate(flops=1024, bytes_accessed=1024, transcendentals=0)
 PARAMS = pltpu.CompilerParams(vmem_limit_bytes=32 * 1024 * 1024)
@@ -67,6 +69,9 @@
         live_list[place] = 0
         dest_list[place] = b
         place = place + lax.rem(place, 2)
+    for n in range(2):
+        chan_list[place + n] = 0
+        src_list[place + n] = 0
     return place // 2
 
 
@@ -75,13 +80,10 @@
     rows = x_ref.shape[1]
     phys = x_ref.shape[2] // LANES
 
-    def step(s, carry):
-        dest = dest_list[2 * s]
-        weights = []
+    def mix(s):
         for i in range(2):
-            k = chan_list[2 * s + i]
             source = src_list[2 * s + i]
-            kron = kron_ref[k]
+            kron = kron_ref[chan_list[2 * s + i]]
             for g in range(rows // (2 * ROWS)):
                 halves = []
                 for j in range(2):
@@ -102,8 +104,13 @@
                         mixed_ref[i, r0 : r0 + ROWS, p * LANES : (p + 1) * LANES] = out[
                             p * ROWS : (p + 1) * ROWS, j * LANES : (j + 1) * LANES
                         ]
-            left = left_ref[k, dest]
-            part = dot(left, mixed_ref[i]).astype(BF16)
+
+    def step(s, carry):
+        dest = dest_list[2 * s]
+        weights = []
+        for i in range(2):
+            k = chan_list[2 * s + i]
+            part = dot(left_ref[k, dest], mixed_ref[i]).astype(BF16)
             for p in range(phys):
                 part_ref[p * rows : (p + 1) * rows, i * LANES : (i + 1) * LANES] = part[
                     :, p * LANES : (p + 1) * LANES
@@ -112,11 +119,13 @@
             if i == 1:
                 right = jnp.where(live_list[2 * s + 1] > 0, right, jnp.zeros_like(right))
             weights.append(right)
+        mix(s + 1)
         image = dot(part_ref[...], jnp.concatenate(weights, axis=0))
         for p in range(phys):
             acc_ref[dest, :, p * LANES : (p + 1) * LANES] += image[p * rows : (p + 1) * rows]
         return carry
 
+    mix(0)
     lax.fori_loop(0, steps, step, 0)
 
 
@@ -128,11 +137,11 @@
 
 
 def row_loop(blocks, rows, body, count):
-    zeros = tuple(jnp.zeros((ROWS, LANES), F32) for _ in range(count))
-    per = rows // ROWS
+    zeros = tuple(jnp.zeros((CHUNK, LANES), F32) for _ in range(count))
+    per = rows // CHUNK
 
     def step(n, carry):
-        return body(n // per, pl.ds(pl.multiple_of(lax.rem(n, per) * ROWS, ROWS), ROWS), carry)
+        return body(n // per, pl.ds(pl.multiple_of(lax.rem(n, per) * CHUNK, CHUNK), CHUNK), carry)
 
     return lax.fori_loop(0, blocks * per, step, zeros)
 
@@ -146,18 +155,27 @@
     return jnp.where(den > 0, num / jnp.where(den > 0, den, 1.0), 0.0)
 
 
+def cut(b, x_ref, out_ref, sem):
+    copy = pltpu.make_async_copy(x_ref.at[pl.ds(b, 1)], out_ref, sem)
+    copy.start()
+    copy.wait()
+
+
 def first_local(
     rel_ref, ops_ref, x_ref, left_ref, right_ref,
     kron_ref, right_t_ref, image_ref, sums_ref,
-    mixed_ref, part_ref, chan_list, src_list, live_list, dest_list,
+    mixed_ref, part_ref, chan_list, src_list, live_list, dest_list, fetched_ref, sem,
 ):
     lists = (chan_list, src_list, live_list, dest_list)
+    fetch = pltpu.make_async_copy(right_ref, fetched_ref, sem)
+    fetch.start()
     make_kron(ops_ref, kron_ref)
     chan, dests = left_ref.shape[:2]
+    fetch.wait()
 
     def turn(n, carry):
         k, b = n // dests, lax.rem(n, dests)
-        right_t_ref[k, b] = right_ref[k, b].T
+        right_t_ref[k, b] = fetched_ref[k, b].T
         return carry
 
     lax.fori_loop(0, chan * dests, turn, 0)
@@ -225,53 +243,43 @@
 
 
 def second_remote(
-    rel_ref, kron_ref, other_ref, left_ref, right_t_ref, before_ref, x_ref, image_ref, remote_ref,
-    mine_ref, theirs_ref,
-    acc_ref, first_ref,
+    rel_ref, kron_ref, other_ref, left_ref, right_t_ref, before_ref,
+    acc_ref,
     mixed_ref, part_ref, chan_list, src_list, live_list, dest_list,
 ):
     lists = (chan_list, src_list, live_list, dest_list)
     dests = left_ref.shape[1]
+    acc_ref[...] = before_ref[...]
+    steps = list_pairs(rel_ref, dests, dests + 1, *lists)
+    add_pairs(steps, lists, kron_ref, other_ref, left_ref, right_t_ref, acc_ref, mixed_ref, part_ref)
+
+
+def second_finish(
+    rel_ref, rank_ref, kron_ref, other_ref, left_ref, right_t_ref, acc_ref, x_ref, image_ref,
+    remote_ref, mine_ref, theirs_ref,
+    kept_ref, kept_first_ref, out_sums_ref,
+    mixed_ref, part_ref, chan_list, src_list, live_list, dest_list,
+):
+    lists = (chan_list, src_list, live_list, dest_list)
+    dests, rows, width = x_ref.shape
+    steps = list_pairs(rel_ref, dests + 1, 2 * dests, *lists)
+    kept_ref[...] = acc_ref[...]
+    add_pairs(steps, lists, kron_ref, other_ref, left_ref, right_t_ref, kept_ref, mixed_ref, part_ref)
     energy = (mine_ref[0:1, :] + theirs_ref[0:1, :]) / (mine_ref[1:2, :] + theirs_ref[1:2, :])
-    times = x_ref.shape[2] // LANES
-    wide = functools.partial(jnp.tile, reps=(1, times))
+    wide = functools.partial(jnp.tile, reps=(1, width // LANES))
     keep_state = wide(1.0 + STEP_SIZE * energy)
     scale_local = wide(STEP_SIZE * (energy - mine_ref[2:3, :]))
     scale_remote = wide(STEP_SIZE * (energy - theirs_ref[2:3, :]))
 
-    def prepare(b, r, carry):
+    def sums(b, r, carry):
         local, remote = image_ref[b, r, :], remote_ref[b, r, :]
         x = x_ref[b, r, :].astype(F32)
-        first_ref[b, r, :] = (keep_state * x - STEP_SIZE * (local + remote)).astype(BF16)
-        acc_ref[b, r, :] = before_ref[b, r, :] + (scale_local * local + scale_remote * remote)
-        return carry
-
-    row_loop(dests, x_ref.shape[1], prepare, 0)
-    steps = list_pairs(rel_ref, dests, dests + 1, *lists)
-    add_pairs(steps, lists, kron_ref, other_ref, left_ref, right_t_ref, acc_ref, mixed_ref, part_ref)
-
-
-def second_finish(
-    rel_ref, rank_ref, kron_ref, other_ref, left_ref, right_t_ref, before_ref, first_ref,
-    mine_ref, theirs_ref,
-    kept_ref, kept_first_ref, out_sums_ref,
-    acc_ref, mixed_ref, part_ref, chan_list, src_list, live_list, dest_list,
-):
-    lists = (chan_list, src_list, live_list, dest_list)
-    dests = left_ref.shape[1]
-    acc_ref[...] = before_ref[...]
-    steps = list_pairs(rel_ref, dests + 1, 2 * dests, *lists)
-    add_pairs(steps, lists, kron_ref, other_ref, left_ref, right_t_ref, acc_ref, mixed_ref, part_ref)
-    energy = (mine_ref[0:1, :] + theirs_ref[0:1, :]) / (mine_ref[1:2, :] + theirs_ref[1:2, :])
-    width = first_ref.shape[2]
-    keep_first = jnp.tile(1.0 + STEP_SIZE * energy, (1, width // LANES))
-
-    def sums(b, r, carry):
-        first = first_ref[b, r, :].astype(F32)
-        image = acc_ref[b, r, :]
-        row = r.start + lax.broadcasted_iota(jnp.int32, (ROWS, width), 0)
+        first_low = (keep_state * x - STEP_SIZE * (local + remote)).astype(BF16)
+        first = first_low.astype(F32)
+        image = kept_ref[b, r, :] + (scale_local * local + scale_remote * remote)
+        row = r.start + lax.broadcasted_iota(jnp.int32, (CHUNK, width), 0)
         mask = row < rank_ref[b]
-        kept = jnp.where(mask, keep_first * first - STEP_SIZE * image, 0.0)
+        kept = jnp.where(mask, keep_state * first - STEP_SIZE * image, 0.0)
         kept_first = jnp.where(mask, first, 0.0)
         kept_ref[b, r, :] = kept
         kept_first_ref[b, r, :] = kept_first.astype(BF16)
@@ -283,7 +291,7 @@
             carry[4] + fold(kept_first * first),
         )
 
-    totals = row_loop(dests, first_ref.shape[1], sums, 5)
+    totals = row_loop(dests, rows, sums, 5)
     for n, total in enumerate(totals):
         out_sums_ref[n : n + 1, :] = jnp.full((1, LANES), 1.0, F32) * jnp.sum(total)
     out_sums_ref[5:6, :] = energy
@@ -318,32 +326,27 @@
     lax.fori_loop(0, blocks * times, turn, 0)
 
 
-def environments(first, count, scale, env_ref, outer_ref, inner_ref, out_ref, mid_ref):
+def environments(first, count, scale, env_ref, inner_ref, outer_ref, out_ref, mid_ref):
     dests, rows, width = outer_ref.shape
     phys = width // LANES
 
     def step(n, carry):
-        pair, b = n // dests, lax.rem(n, dests)
-        k = first + 2 * pair
-        env = jnp.concatenate([env_ref[k, b], env_ref[k + 1, b]], axis=1)
-        tall = jnp.concatenate(
-            [outer_ref[b, :, p * LANES : (p + 1) * LANES] for p in range(phys)], axis=0
-        )
-        mid = dot(tall, env).astype(BF16)
-        for p in range(phys):
-            for i in range(2):
-                mid_ref[i * rows : (i + 1) * rows, p * LANES : (p + 1) * LANES] = mid[
-                    p * rows : (p + 1) * rows, i * LANES : (i + 1) * LANES
-                ]
-        last = jnp.concatenate(
-            [inner_ref[b, :, p * LANES : (p + 1) * LANES] for p in range(phys)], axis=0
-        )
-        out = (dot(mid_ref[...], last) * scale).astype(BF16)
-        out_ref[2 * pair, b] = out[:rows]
-        out_ref[2 * pair + 1, b] = out[rows:]
+        k = first + 2 * n
+        for b in range(dests):
+            env = jnp.concatenate([env_ref[k, b], env_ref[k + 1, b]], axis=0)
+            mid = dot(env, inner_ref[b]).astype(BF16)
+            for p in range(phys):
+                for i in range(2):
+                    mid_ref[b, p * rows : (p + 1) * rows, i * LANES : (i + 1) * LANES] = mid[
+                        i * rows : (i + 1) * rows, p * LANES : (p + 1) * LANES
+                    ]
+        for b in range(dests):
+            out = (dot(outer_ref[b], mid_ref[b]) * scale).astype(BF16)
+            out_ref[2 * n, b] = out[:, :LANES]
+            out_ref[2 * n + 1, b] = out[:, LANES:]
         return carry
 
-    lax.fori_loop(0, (count // 2) * dests, step, 0)
+    lax.fori_loop(0, count // 2, step, 0)
 
 
 def normalize_and_left(
@@ -355,7 +358,7 @@
     normalize(cells, kept_ref, first_ref, mine_ref, theirs_ref, state_ref, turned_ref)
     copy = pltpu.make_async_copy(state_ref, new_ref, sem)
     copy.start()
-    environments(first, count, scale, env_ref, turned_ref, state_ref, out_ref, mid_ref)
+    environments(first, count, scale, env_ref, state_ref, turned_ref, out_ref, mid_ref)
     copy.wait()
 
 
@@ -416,11 +419,18 @@
             cost_estimate=COST,
         )(*args)
 
-    other = [trade(x[b : b + 1]) for b in range(dests)]
+    def block_of(b):
+        return call(
+            functools.partial(cut, b), [HBM], shape((1, rows, width), BF16),
+            [pltpu.SemaphoreType.DMA], x,
+        )
+
+    other = [trade(block_of(b)) for b in range(dests)]
     kron, right_t, image_local, sums_local = call(
-        first_local, [SMEM] + [VMEM] * 4,
+        first_local, [SMEM] + [VMEM] * 3 + [HBM],
         (shape((chan, phys * ROWS, phys * ROWS), BF16), shape(right.shape, BF16), wave_f32, sums_kind),
-        pair_scratch, rel, ops, x, left, right,
+        pair_scratch + [pltpu.VMEM(right.shape, BF16), pltpu.SemaphoreType.DMA],
+        rel, ops, x, left, right,
     )
     image_remote = call(
         first_remote, [SMEM] + [VMEM] * 4, wave_f32, pair_scratch,
@@ -436,21 +446,21 @@
         second_local, [SMEM] + [VMEM] * 4, wave_f32, pair_scratch,
         rel, kron, guess, left, right_t,
     )
-    acc, first = call(
-        second_remote, [SMEM] + [VMEM] * 10, (wave_f32, wave_b16), pair_scratch,
-        rel, kron, other[0], left, right_t, acc, x, image_local, image_remote, mine, theirs,
+    acc = call(
+        second_remote, [SMEM] + [VMEM] * 5, wave_f32, pair_scratch,
+        rel, kron, other[0], left, right_t, acc,
     )
     kept, kept_first, sums_mine = call(
-        second_finish, [SMEM, SMEM] + [VMEM] * 8, (wave_f32, wave_b16, sums_kind),
-        [pltpu.VMEM(wave, F32)] + pair_scratch,
-        rel, ranks[0], kron, other[1], left, right_t, acc, first, mine, theirs,
+        second_finish, [SMEM, SMEM] + [VMEM] * 10, (wave_f32, wave_b16, sums_kind), pair_scratch,
+        rel, ranks[0], kron, other[1], left, right_t, acc, x, image_local, image_remote,
+        mine, theirs,
     )
     sums_theirs = trade(sums_mine)
 
     env_scale = 1.0 / math.sqrt(phys * rows)
     cells = float(total_blocks * rows * width)
     early, later = 10, 8
-    mid = [pltpu.VMEM((2 * rows, width), BF16)]
+    mid = [pltpu.VMEM((dests, width, 2 * LANES), BF16)]
 
     def sent(value, steps):
         count = lax.axis_size("seg")
@@ -460,16 +470,16 @@
     def env_kind(count):
         return shape((count,) + left.shape[1:], BF16)
 
-    def env_call(begin, count, env, outer, inner):
+    def env_call(begin, count, env, inner, outer):
         return call(
             functools.partial(environments, begin, count, env_scale),
-            [VMEM] * 3, env_kind(count), mid, env, outer, inner,
+            [VMEM] * 3, env_kind(count), mid, env, inner, outer,
         )
 
     new_state, state_kept, turned, piece = pl.pallas_call(
         functools.partial(normalize_and_left, 0, early, env_scale, cells),
         in_specs=[VMEM] * 5,
-        out_specs=(pl.BlockSpec(memory_space=pltpu.HBM), VMEM, VMEM, VMEM),
+        out_specs=(HBM, VMEM, VMEM, VMEM),
         out_shape=(wave_b16, wave_b16, wave_b16, env_kind(early)),
         scratch_shapes=mid + [pltpu.SemaphoreType.DMA],
         compiler_params=PARAMS,
@@ -477,15 +487,15 @@
     )(kept, kept_first, sums_mine, sums_theirs, left)
     lefts = [sent(piece, 1)]
     rights = [
-        sent(env_call(0, later, right, state_kept, turned), -1),
-        sent(env_call(later, chan - later, right, state_kept, turned), -1),
+        sent(env_call(0, later, right, turned, state_kept), -1),
+        sent(env_call(later, chan - later, right, turned, state_kept), -1),
     ]
-    lefts.append(sent(env_call(early, chan - early, left, turned, state_kept), 1))
+    lefts.append(sent(env_call(early, chan - early, left, state_kept, turned), 1))
     env_f32 = shape(left.shape, F32)
     received_left, received_right = pl.pallas_call(
         functools.partial(widen, ((0, 0), (1, 0), (1, later), (0, early))),
         in_specs=[VMEM] * 4,
-        out_specs=(pl.BlockSpec(memory_space=pltpu.HBM),) * 2,
+        out_specs=(HBM,) * 2,
         out_shape=(env_f32, env_f32),
         scratch_shapes=[pltpu.VMEM(left.shape, F32)] * 2 + [pltpu.SemaphoreType.DMA((4,))],
         compiler_params=PARAMS,

time: 129 us -> 109 us (0.84); the launches traced: 127 us -> 110 us
  Pallas kernels: 86.9 us -> 70.9 us
  local copies, waits for them, and re-layouts: 3.81 us -> 1.52 us
  waiting for transfers between devices: 15.7 us -> 17.2 us
    pallas_call x9 -> x11, Pallas kernels: 72.4 us -> 61 us  [call(): pl.pallas_call(body, in_specs=specs, out_specs=jax.tree.map(lambda _: VME...]
    ppermute x4, waiting for transfers between devices: 3.3 us -> 9.64 us  [sent(): lax.ppermute(value, 'seg', [(s, s + steps) for s in range(begin, end)])]
    ppermute x4, starting transfers between devices: 15.7 us -> 10.8 us  [sent(): lax.ppermute(value, 'seg', [(s, s + steps) for s in range(begin, end)])]
    ppermute x6, starting transfers between devices: 3.87 us -> 8.72 us  [trade(): return lax.ppermute(value, 'blk', swap)]
    ppermute x6, waiting for transfers between devices: 12.4 us -> 7.58 us  [trade(): return lax.ppermute(value, 'blk', swap)]
    pallas_call x1, Pallas kernels: 12.5 us -> 7.91 us  [shards(): pl.pallas_call(functools.partial(normalize_and_left, 0, early, env_scale,...]
    slice x1 -> x0, local copies, waits for them, and re-layouts: 2.41 us -> none  [shards(): other = [trade(x[b:b + 1]) for b in range(dests)]]
  transfers between devices with their start and end apart: 10 -> 10, of which waited for: 3 -> 4; matrix products, arithmetic and copies ran while one was open for 0% -> 0% of each run, Pallas kernels for 46% -> 44%
where the time goes in v2:
time: 109 us; the launch traced here: 110 us
  Pallas kernels  70.9 us (65%)
  starting transfers between devices  19.5 us (18%)
  waiting for transfers between devices  17.2 us (16%)
  local copies, waits for them, and re-layouts  1.52 us (1%)
    pallas_call x11, Pallas kernels, call(): pl.pallas_call(body, in_specs=specs, out_specs=jax.tree.map(lambda _: VME...  61 us
    ppermute x4, starting transfers between devices, sent(): lax.ppermute(value, 'seg', [(s, s + steps) for s in range(begin, end)])  10.8 us
    ppermute x4, waiting for transfers between devices, sent(): lax.ppermute(value, 'seg', [(s, s + steps) for s in range(begin, end)])  9.64 us
    ppermute x6, starting transfers between devices, trade(): return lax.ppermute(value, 'blk', swap)  8.72 us
    pallas_call x1, Pallas kernels, shards(): pl.pallas_call(functools.partial(normalize_and_left, 0, early, env_scale,...  7.91 us
    ppermute x6, waiting for transfers between devices, trade(): return lax.ppermute(value, 'blk', swap)  7.58 us
  transfers between devices with their start and end apart: 10, of which 4 were waited for; matrix products, arithmetic and copies ran while one was open for 0% of the time, Pallas kernels for 44%

profile of v2, /device:TPU:1, one launch (start us, length us, event | category | flops | bytes accessed | tf_op | source)
XLA Modules:
  0.0 110.1 jit_solution(1813809469398413192)
XLA Ops:
  0.6 0.0 copy-start
  0.6 0.0 copy-start.1
  0.7 1.3 %copy-done.1 = bf16[1,2,128,2048]{3,2,1,0:T(8,128)(2,1)S(1)} copy-done((bf16[1,2,128,2048]{3,2,1,0:T(8,128)(2,1)S(1)}, bf16[1,2,128,2048]{3,2,1,0:T(8,128)(2,1)}, u32[]{:S(2)}) %copy-start.1) | copy-done | bytes 1048600
  1.9 0.0 copy-start.6
  1.9 0.0 copy-start.2
  2.0 0.0 copy-start.3
  2.0 0.0 copy-start.4
  2.0 0.8 shard_map.87
  2.8 2.1 %collective-permute-start.1 = (bf16[1,128,2048]{2,1,0:T(8,128)(2,1)}, bf16[1,128,2048]{2,1,0:T(8,128)(2,1)}, u32[]{:S(2)}, u32[]{:S(2)}) collective-permute-start(bf16[1,128,2048]{2,1,0:T(8,128)(2,1)} %shard_map.87), channel_id=1, source_target_pairs={{0,1},{1,0},{2,3},{3,2},{4,5},{5,4},{6,7},{7,6},{8,9},{9,8},{10,11... | collective-permute-start | bytes 1572872 | tf_op jit(solution)/shard_map/ppermute | solution.py:397
  4.9 0.8 shard_map.86
  5.8 0.1 collective-permute-start
  5.8 0.0 copy-done.6
  5.9 0.1 copy.9
  6.0 0.0 copy-done
  6.0 0.0 copy-done.2
  6.0 0.0 copy-done.3
  6.0 0.0 copy-done.4
  6.0 17.7 %shard_map.85 = (bf16[14,256,256]{2,1,0:T(8,128)(2,1)S(1)}, bf16[14,2,128,128]{3,2,1,0:T(8,128)(2,1)S(1)}, f32[2,128,2048]{2,1,0:T(8,128)S(1)}, f32[8,128]{1,0:T(8,128)S(1)}) custom-call(s32[14,2]{1,0:T(8,128)S(1)} %negate_select_fusion.rel_ref, bf16[14,16,16]{2,1,0:T(8,128)(2,1)S(1)} %bitcast.26, bf16[2,128,2048]{2,1,0:T(8,128)(2,1)S(1)} %bitcast.20, ...), custom_call_target="tpu_custom_call" | custom-call | flops 1024 | bytes 1024 | tf_op jit(solution)/shard_map/pallas_call | solution.py:412
  23.7 0.0 collective-permute-done.1.other_ref
  23.7 5.7 %shard_map.88.before_ref = f32[2,128,2048]{2,1,0:T(8,128)S(1)} custom-call(s32[14,2]{1,0:T(8,128)S(1)} %negate_select_fusion.rel_ref, bf16[14,256,256]{2,1,0:T(8,128)(2,1)S(1)} %get-tuple-element.19.kron_ref, bf16[1,128,2048]{2,1,0:T(8,128)(2,1)} %collective-permute-done.1.other_ref, bf16[14,2,128,128]{3,2,1,0:T(8,128)(2,1)S(1)} %bitcast.11, ...), custom_call_target="tpu_custom_call" | custom-call | flops 1024 | bytes 1024 | tf_op jit(solution)/shard_map/pallas_call | solution.py:412
  29.4 0.0 collective-permute-done.other_ref
  29.4 5.0 %shard_map.89 = (f32[2,128,2048]{2,1,0:T(8,128)S(1)}, bf16[2,128,2048]{2,1,0:T(8,128)(2,1)S(1)}, f32[8,128]{1,0:T(8,128)S(1)}) custom-call(s32[14,2]{1,0:T(8,128)S(1)} %negate_select_fusion.rel_ref, bf16[14,256,256]{2,1,0:T(8,128)(2,1)S(1)} %get-tuple-element.19.kron_ref, bf16[1,128,2048]{2,1,0:T(8,128)(2,1)S(1)} %collective-permute-done.other_ref, ...), custom_call_target="tpu_custom_call" | custom-call | flops 1024 | bytes 1024 | tf_op jit(solution)/shard_map/pallas_call | solution.py:412
  34.4 0.1 fusion.1
  34.5 1.8 %collective-permute-start.3 = (bf16[1,128,2048]{2,1,0:T(8,128)(2,1)S(1)}, bf16[1,128,2048]{2,1,0:T(8,128)(2,1)S(1)}, u32[]{:S(2)}, u32[]{:S(2)}) collective-permute-start(bf16[1,128,2048]{2,1,0:T(8,128)(2,1)S(1)} %get-tuple-element.35), channel_id=1, source_target_pairs={{0,1},{1,0},{2,3},{3,2},{4,5},{5,4},{6,7},{7,6},{8,9},{9,8},{10,11... | collective-permute-start | bytes 1572872 | tf_op jit(solution)/shard_map/ppermute | solution.py:397
  36.3 0.1 collective-permute-start.2
  36.4 1.4 %collective-permute-start.4 = (f32[8,128]{1,0:T(8,128)S(1)}, f32[8,128]{1,0:T(8,128)S(1)}, u32[]{:S(2)}, u32[]{:S(2)}) collective-permute-start(f32[8,128]{1,0:T(8,128)S(1)} %get-tuple-element.25.mine_ref), channel_id=1, source_target_pairs={{0,1},{1,0},{2,3},{3,2},{4,5},{5,4},{6,7},{7,6},{8,9},{9,8},{10,11... | collective-permute-start | bytes 12296 | tf_op jit(solution)/shard_map/ppermute | solution.py:397
  37.8 10.4 %shard_map.90.before_ref = f32[2,128,2048]{2,1,0:T(8,128)S(1)} custom-call(s32[14,2]{1,0:T(8,128)S(1)} %negate_select_fusion.rel_ref, bf16[14,256,256]{2,1,0:T(8,128)(2,1)S(1)} %get-tuple-element.19.kron_ref, bf16[2,128,2048]{2,1,0:T(8,128)(2,1)S(1)} %get-tuple-element.23.guess_ref, bf16[14,2,128,128]{3,2,1,0:T(8,128)(2,1)S(1)} %bitcast.13, ...), custom_call_target="tpu_custom_call" | custom-call | flops 1024 | bytes 1024 | tf_op jit(solution)/shard_map/pallas_call | solution.py:412
  48.1 0.0 copy-start.5
  48.2 0.5 collective-permute-done.3.other_ref
  48.7 5.2 %shard_map.91.acc_ref = f32[2,128,2048]{2,1,0:T(8,128)S(1)} custom-call(s32[14,2]{1,0:T(8,128)S(1)} %negate_select_fusion.rel_ref, bf16[14,256,256]{2,1,0:T(8,128)(2,1)S(1)} %get-tuple-element.19.kron_ref, bf16[1,128,2048]{2,1,0:T(8,128)(2,1)S(1)} %collective-permute-done.3.other_ref, bf16[14,2,128,128]{3,2,1,0:T(8,128)(2,1)S(1)} %bitcast.14, ...), custom_call_target="tpu_custom_call" | custom-call | flops 1024 | bytes 1024 | tf_op jit(solution)/shard_map/pallas_call | solution.py:412
  53.9 6.1 %collective-permute-done.4.theirs_ref = f32[8,128]{1,0:T(8,128)S(1)} collective-permute-done((f32[8,128]{1,0:T(8,128)S(1)}, f32[8,128]{1,0:T(8,128)S(1)}, u32[]{:S(2)}, u32[]{:S(2)}) %collective-permute-start.4) | collective-permute-done | bytes 4128 | tf_op jit(solution)/shard_map/ppermute | solution.py:397
  60.0 0.0 collective-permute-done.2.other_ref
  60.0 0.0 copy-done.5
  60.0 6.2 %shard_map.92 = (f32[2,128,2048]{2,1,0:T(8,128)S(1)}, bf16[2,128,2048]{2,1,0:T(8,128)(2,1)S(1)}, f32[8,128]{1,0:T(8,128)S(1)}) custom-call(s32[14,2]{1,0:T(8,128)S(1)} %negate_select_fusion.rel_ref, s32[2]{0:T(128)S(1)} %bitcast.27, bf16[14,256,256]{2,1,0:T(8,128)(2,1)S(1)} %get-tuple-element.19.kron_ref, ...), custom_call_target="tpu_custom_call" | custom-call | flops 1024 | bytes 1024 | tf_op jit(solution)/shard_map/pallas_call | solution.py:412
  66.2 3.3 %collective-permute-start.5 = (f32[8,128]{1,0:T(8,128)S(1)}, f32[8,128]{1,0:T(8,128)S(1)}, u32[]{:S(2)}, u32[]{:S(2)}) collective-permute-start(f32[8,128]{1,0:T(8,128)S(1)} %get-tuple-element.28.mine_ref), channel_id=1, source_target_pairs={{0,1},{1,0},{2,3},{3,2},{4,5},{5,4},{6,7},{7,6},{8,9},{9,8},{10,11... | collective-permute-start | bytes 12296 | tf_op jit(solution)/shard_map/ppermute | solution.py:397
  69.5 1.0 collective-permute-done.5.theirs_ref
  70.5 7.9 %shard_map.93 = (bf16[2,128,2048]{2,1,0:T(8,128)(2,1)}, bf16[2,128,2048]{2,1,0:T(8,128)(2,1)S(1)}, bf16[2,128,2048]{2,1,0:T(8,128)(2,1)S(1)}, bf16[10,2,128,128]{3,2,1,0:T(8,128)(2,1)S(1)}) custom-call(f32[2,128,2048]{2,1,0:T(8,128)S(1)} %get-tuple-element.26.kept_ref, bf16[2,128,2048]{2,1,0:T(8,128)(2,1)S(1)} %get-tuple-element.27.first_ref, ...), custom_call_target="tpu_custom_call" | custom-call | flops 1024 | bytes 1024 | tf_op jit(solution)/shard_map/pallas_call | solution.py:479
  78.4 3.3 %collective-permute-start.6 = (bf16[10,2,128,128]{3,2,1,0:T(8,128)(2,1)S(1)}, bf16[10,2,128,128]{3,2,1,0:T(8,128)(2,1)S(1)}, u32[]{:S(2)}, u32[]{:S(2)}) collective-permute-start(bf16[10,2,128,128]{3,2,1,0:T(8,128)(2,1)S(1)} %get-tuple-element.30), channel_id=1, source_target_pairs={{0,2},{2,4},{4,6},{6,8},{8,10},{10,12},{12,14},{14,16},{16,18},{18... | collective-permute-start | bytes 1966088 | tf_op jit(solution)/shard_map/ppermute | solution.py:468
  81.8 4.1 %shard_map.94 = bf16[8,2,128,128]{3,2,1,0:T(8,128)(2,1)S(1)} custom-call(bf16[14,2,128,128]{3,2,1,0:T(8,128)(2,1)S(1)} %bitcast.24, bf16[2,128,2048]{2,1,0:T(8,128)(2,1)S(1)} %get-tuple-element.31.inner_ref.outer_ref, bf16[2,128,2048]{2,1,0:T(8,128)(2,1)S(1)} %get-tuple-element.32.outer_ref.inner_ref), custom_call_target="tpu_custom_call" | custom-call | flops 1024 | bytes 1024 | tf_op jit(solution)/shard_map/pallas_call | solution.py:412
  85.8 1.9 %collective-permute-start.7 = (bf16[8,2,128,128]{3,2,1,0:T(8,128)(2,1)S(1)}, bf16[8,2,128,128]{3,2,1,0:T(8,128)(2,1)S(1)}, u32[]{:S(2)}, u32[]{:S(2)}) collective-permute-start(bf16[8,2,128,128]{3,2,1,0:T(8,128)(2,1)S(1)} %shard_map.94), channel_id=1, source_target_pairs={{2,0},{4,2},{6,4},{8,6},{10,8},{12,10},{14,12},{16,14},{18,16},{20... | collective-permute-start | bytes 1572872 | tf_op jit(solution)/shard_map/ppermute | solution.py:468
  87.8 3.1 %shard_map.95 = bf16[6,2,128,128]{3,2,1,0:T(8,128)(2,1)S(1)} custom-call(bf16[14,2,128,128]{3,2,1,0:T(8,128)(2,1)S(1)} %bitcast.25, bf16[2,128,2048]{2,1,0:T(8,128)(2,1)S(1)} %get-tuple-element.31.inner_ref.outer_ref, bf16[2,128,2048]{2,1,0:T(8,128)(2,1)S(1)} %get-tuple-element.32.outer_ref.inner_ref), custom_call_target="tpu_custom_call" | custom-call | flops 1024 | bytes 1024 | tf_op jit(solution)/shard_map/pallas_call | solution.py:412
  90.8 1.9 %collective-permute-start.8 = (bf16[6,2,128,128]{3,2,1,0:T(8,128)(2,1)S(1)}, bf16[6,2,128,128]{3,2,1,0:T(8,128)(2,1)S(1)}, u32[]{:S(2)}, u32[]{:S(2)}) collective-permute-start(bf16[6,2,128,128]{3,2,1,0:T(8,128)(2,1)S(1)} %shard_map.95), channel_id=1, source_target_pairs={{2,0},{4,2},{6,4},{8,6},{10,8},{12,10},{14,12},{16,14},{18,16},{20... | collective-permute-start | bytes 1179656 | tf_op jit(solution)/shard_map/ppermute | solution.py:468
  92.8 2.0 %shard_map.96 = bf16[4,2,128,128]{3,2,1,0:T(8,128)(2,1)S(1)} custom-call(bf16[14,2,128,128]{3,2,1,0:T(8,128)(2,1)S(1)} %bitcast.17, bf16[2,128,2048]{2,1,0:T(8,128)(2,1)S(1)} %get-tuple-element.32.outer_ref.inner_ref, bf16[2,128,2048]{2,1,0:T(8,128)(2,1)S(1)} %get-tuple-element.31.inner_ref.outer_ref), custom_call_target="tpu_custom_call" | custom-call | flops 1024 | bytes 1024 | tf_op jit(solution)/shard_map/pallas_call | solution.py:412
  94.8 3.6 %collective-permute-start.9 = (bf16[4,2,128,128]{3,2,1,0:T(8,128)(2,1)S(1)}, bf16[4,2,128,128]{3,2,1,0:T(8,128)(2,1)S(1)}, u32[]{:S(2)}, u32[]{:S(2)}) collective-permute-start(bf16[4,2,128,128]{3,2,1,0:T(8,128)(2,1)S(1)} %shard_map.96), channel_id=1, source_target_pairs={{0,2},{2,4},{4,6},{6,8},{8,10},{10,12},{12,14},{14,16},{16,18},{18... | collective-permute-start | bytes 786440 | tf_op jit(solution)/shard_map/ppermute | solution.py:468
  98.5 9.6 %collective-permute-done.9.refs_3_ = bf16[4,2,128,128]{3,2,1,0:T(8,128)(2,1)S(1)} collective-permute-done((bf16[4,2,128,128]{3,2,1,0:T(8,128)(2,1)S(1)}, bf16[4,2,128,128]{3,2,1,0:T(8,128)(2,1)S(1)}, u32[]{:S(2)}, u32[]{:S(2)}) %collective-permute-start.9) | collective-permute-done | bytes 262176 | tf_op jit(solution)/shard_map/ppermute | solution.py:468
  108.1 0.0 collective-permute-done.8.refs_2_
  108.1 0.0 collective-permute-done.7.refs_1_
  108.1 0.0 collective-permute-done.6.refs_0_
  108.1 2.0 %shard_map.97 = (f32[14,2,128,128]{3,2,1,0:T(8,128)}, f32[14,2,128,128]{3,2,1,0:T(8,128)}) custom-call(bf16[10,2,128,128]{3,2,1,0:T(8,128)(2,1)S(1)} %collective-permute-done.6.refs_0_, bf16[8,2,128,128]{3,2,1,0:T(8,128)(2,1)S(1)} %collective-permute-done.7.refs_1_, bf16[6,2,128,128]{3,2,1,0:T(8,128)(2,1)S(1)} %collective-permute-done.8.refs_2_, ...), custom_call_target="tpu_custom_call" | custom-call | flops 1024 | bytes 1024 | tf_op jit(solution)/shard_map/pallas_call | solution.py:495
  (2 shorter events, 0.0 us)
Async XLA Ops:
  0.6 5.3 %copy-start = (bf16[1,14,2,128,128]{4,3,2,1,0:T(8,128)(2,1)S(1)}, bf16[1,14,2,128,128]{4,3,2,1,0:T(8,128)(2,1)}, u32[]{:S(2)}) copy-start(bf16[1,14,2,128,128]{4,3,2,1,0:T(8,128)(2,1)} %param.7) | copy-start | bytes 2752516
  0.6 1.3 %copy-start.1 = (bf16[1,2,128,2048]{3,2,1,0:T(8,128)(2,1)S(1)}, bf16[1,2,128,2048]{3,2,1,0:T(8,128)(2,1)}, u32[]{:S(2)}) copy-start(bf16[1,2,128,2048]{3,2,1,0:T(8,128)(2,1)} %param.6) | copy-start | bytes 3145732
  1.9 3.9 %copy-start.6 = (s32[1,14,4]{1,2,0:T(4,128)S(1)}, s32[1,14,4]{1,2,0:T(4,128)}, u32[]{:S(2)}) copy-start(s32[1,14,4]{1,2,0:T(4,128)} %param.10) | copy-start | bytes 676
  1.9 4.0 %copy-start.2 = (bf16[1,2,128,2048]{3,2,1,0:T(8,128)(2,1)S(1)}, bf16[1,2,128,2048]{3,2,1,0:T(8,128)(2,1)}, u32[]{:S(2)}) copy-start(bf16[1,2,128,2048]{3,2,1,0:T(8,128)(2,1)} %param.6) | copy-start | bytes 3145732
  2.0 4.0 %copy-start.3 = (bf16[1,14,2,128,128]{4,3,2,1,0:T(8,128)(2,1)S(1)}, bf16[1,14,2,128,128]{4,3,2,1,0:T(8,128)(2,1)}, u32[]{:S(2)}) copy-start(bf16[1,14,2,128,128]{4,3,2,1,0:T(8,128)(2,1)} %param.8) | copy-start | bytes 2752516
  2.0 4.0 %copy-start.4 = (bf16[1,14,16,16]{3,2,1,0:T(8,128)(2,1)S(1)}, bf16[1,14,16,16]{3,2,1,0:T(8,128)(2,1)}, u32[]{:S(2)}) copy-start(bf16[1,14,16,16]{3,2,1,0:T(8,128)(2,1)} %param.9) | copy-start | bytes 21508
  2.8 20.9 %collective-permute-start.1 = (bf16[1,128,2048]{2,1,0:T(8,128)(2,1)}, bf16[1,128,2048]{2,1,0:T(8,128)(2,1)}, u32[]{:S(2)}, u32[]{:S(2)}) collective-permute-start(bf16[1,128,2048]{2,1,0:T(8,128)(2,1)} %shard_map.87), channel_id=1, source_target_pairs={{0,1},{1,0},{2,3},{3,2},{4,5},{5,4},{6,7},{7,6},{8,9},{9,8},{10,11... | collective-permute-start | bytes 1572872 | tf_op jit(solution)/shard_map/ppermute | solution.py:397
  5.8 23.6 %collective-permute-start = (bf16[1,128,2048]{2,1,0:T(8,128)(2,1)}, bf16[1,128,2048]{2,1,0:T(8,128)(2,1)S(1)}, u32[]{:S(2)}, u32[]{:S(2)}) collective-permute-start(bf16[1,128,2048]{2,1,0:T(8,128)(2,1)} %shard_map.86), channel_id=1, source_target_pairs={{0,1},{1,0},{2,3},{3,2},{4,5},{5,4},{6,7},{7,6},{8,9},{9,8},{10,11... | collective-permute-start | bytes 1572872 | tf_op jit(solution)/shard_map/ppermute | solution.py:397
  34.5 14.1 %collective-permute-start.3 = (bf16[1,128,2048]{2,1,0:T(8,128)(2,1)S(1)}, bf16[1,128,2048]{2,1,0:T(8,128)(2,1)S(1)}, u32[]{:S(2)}, u32[]{:S(2)}) collective-permute-start(bf16[1,128,2048]{2,1,0:T(8,128)(2,1)S(1)} %get-tuple-element.35), channel_id=1, source_target_pairs={{0,1},{1,0},{2,3},{3,2},{4,5},{5,4},{6,7},{7,6},{8,9},{9,8},{10,11... | collective-permute-start | bytes 1572872 | tf_op jit(solution)/shard_map/ppermute | solution.py:397
  36.3 23.7 %collective-permute-start.2 = (bf16[1,128,2048]{2,1,0:T(8,128)(2,1)S(1)}, bf16[1,128,2048]{2,1,0:T(8,128)(2,1)S(1)}, u32[]{:S(2)}, u32[]{:S(2)}) collective-permute-start(bf16[1,128,2048]{2,1,0:T(8,128)(2,1)S(1)} %get-tuple-element.36), channel_id=1, source_target_pairs={{0,1},{1,0},{2,3},{3,2},{4,5},{5,4},{6,7},{7,6},{8,9},{9,8},{10,11... | collective-permute-start | bytes 1572872 | tf_op jit(solution)/shard_map/ppermute | solution.py:397
  36.4 23.6 %collective-permute-start.4 = (f32[8,128]{1,0:T(8,128)S(1)}, f32[8,128]{1,0:T(8,128)S(1)}, u32[]{:S(2)}, u32[]{:S(2)}) collective-permute-start(f32[8,128]{1,0:T(8,128)S(1)} %get-tuple-element.25.mine_ref), channel_id=1, source_target_pairs={{0,1},{1,0},{2,3},{3,2},{4,5},{5,4},{6,7},{7,6},{8,9},{9,8},{10,11... | collective-permute-start | bytes 12296 | tf_op jit(solution)/shard_map/ppermute | solution.py:397
  48.1 11.8 %copy-start.5 = (s32[1,2]{1,0:T(1,128)S(1)}, s32[1,2]{1,0:T(1,128)}, u32[]{:S(2)}) copy-start(s32[1,2]{1,0:T(1,128)} %param.11) | copy-start | bytes 28
  66.2 4.3 %collective-permute-start.5 = (f32[8,128]{1,0:T(8,128)S(1)}, f32[8,128]{1,0:T(8,128)S(1)}, u32[]{:S(2)}, u32[]{:S(2)}) collective-permute-start(f32[8,128]{1,0:T(8,128)S(1)} %get-tuple-element.28.mine_ref), channel_id=1, source_target_pairs={{0,1},{1,0},{2,3},{3,2},{4,5},{5,4},{6,7},{7,6},{8,9},{9,8},{10,11... | collective-permute-start | bytes 12296 | tf_op jit(solution)/shard_map/ppermute | solution.py:397
  78.4 29.7 %collective-permute-start.6 = (bf16[10,2,128,128]{3,2,1,0:T(8,128)(2,1)S(1)}, bf16[10,2,128,128]{3,2,1,0:T(8,128)(2,1)S(1)}, u32[]{:S(2)}, u32[]{:S(2)}) collective-permute-start(bf16[10,2,128,128]{3,2,1,0:T(8,128)(2,1)S(1)} %get-tuple-element.30), channel_id=1, source_target_pairs={{0,2},{2,4},{4,6},{6,8},{8,10},{10,12},{12,14},{14,16},{16,18},{18... | collective-permute-start | bytes 1966088 | tf_op jit(solution)/shard_map/ppermute | solution.py:468
  85.8 22.2 %collective-permute-start.7 = (bf16[8,2,128,128]{3,2,1,0:T(8,128)(2,1)S(1)}, bf16[8,2,128,128]{3,2,1,0:T(8,128)(2,1)S(1)}, u32[]{:S(2)}, u32[]{:S(2)}) collective-permute-start(bf16[8,2,128,128]{3,2,1,0:T(8,128)(2,1)S(1)} %shard_map.94), channel_id=1, source_target_pairs={{2,0},{4,2},{6,4},{8,6},{10,8},{12,10},{14,12},{16,14},{18,16},{20... | collective-permute-start | bytes 1572872 | tf_op jit(solution)/shard_map/ppermute | solution.py:468
  90.8 17.3 %collective-permute-start.8 = (bf16[6,2,128,128]{3,2,1,0:T(8,128)(2,1)S(1)}, bf16[6,2,128,128]{3,2,1,0:T(8,128)(2,1)S(1)}, u32[]{:S(2)}, u32[]{:S(2)}) collective-permute-start(bf16[6,2,128,128]{3,2,1,0:T(8,128)(2,1)S(1)} %shard_map.95), channel_id=1, source_target_pairs={{2,0},{4,2},{6,4},{8,6},{10,8},{12,10},{14,12},{16,14},{18,16},{20... | collective-permute-start | bytes 1179656 | tf_op jit(solution)/shard_map/ppermute | solution.py:468
  94.8 13.3 %collective-permute-start.9 = (bf16[4,2,128,128]{3,2,1,0:T(8,128)(2,1)S(1)}, bf16[4,2,128,128]{3,2,1,0:T(8,128)(2,1)S(1)}, u32[]{:S(2)}, u32[]{:S(2)}) collective-permute-start(bf16[4,2,128,128]{3,2,1,0:T(8,128)(2,1)S(1)} %shard_map.96), channel_id=1, source_target_pairs={{0,2},{2,4},{4,6},{6,8},{8,10},{10,12},{12,14},{14,16},{16,18},{18... | collective-permute-start | bytes 786440 | tf_op jit(solution)/shard_map/ppermute | solution.py:468

commit v3 on v2

--- a/solution.py
+++ b/solution.py
@@ -28,35 +28,30 @@
     )
 
 
-def make_kron(ops_ref, kron_ref):
+def make_kron(ops_ref, kron_ref, spread_ref):
     chan, phys, _ = ops_ref.shape
     wide = phys * ROWS
-    spread_rows = (
-        lax.broadcasted_iota(jnp.int32, (wide, phys), 0) // ROWS
-        == lax.broadcasted_iota(jnp.int32, (wide, phys), 1)
-    ).astype(F32).astype(BF16)
-    spread_cols = (
-        lax.broadcasted_iota(jnp.int32, (phys, wide), 1) // ROWS
-        == lax.broadcasted_iota(jnp.int32, (phys, wide), 0)
-    ).astype(F32).astype(BF16)
-    diagonal = (
-        lax.broadcasted_iota(jnp.int32, (wide, wide), 0) % ROWS
-        == lax.broadcasted_iota(jnp.int32, (wide, wide), 1) % ROWS
+    columns = lax.broadcasted_iota(jnp.int32, (phys, wide), 1)
+    spread = (columns // ROWS == lax.broadcasted_iota(jnp.int32, (phys, wide), 0)).astype(F32)
+    spread_ref[...] = dot(ops_ref[...].reshape(chan * phys, phys), spread.astype(BF16))
+    same = lax.broadcasted_iota(jnp.int32, (ROWS, wide), 1) % ROWS == lax.broadcasted_iota(
+        jnp.int32, (ROWS, wide), 0
     )
 
     def one(k, carry):
-        tall = dot(spread_rows, ops_ref[k]).astype(BF16)
-        full = dot(tall, spread_cols)
-        kron_ref[k] = jnp.where(diagonal, full, 0.0).astype(BF16)
+        rows = spread_ref[pl.ds(pl.multiple_of(k * phys, phys), phys), :]
+        for p in range(phys):
+            full = jnp.broadcast_to(rows[p : p + 1], (ROWS, wide))
+            kron_ref[k, p * ROWS : (p + 1) * ROWS, :] = jnp.where(same, full, 0.0).astype(BF16)
         return carry
 
     lax.fori_loop(0, chan, one, 0)
 
 
-def list_pairs(rel_ref, low, high, chan_list, src_list, live_list, dest_list):
+def list_pairs(rel_ref, low, high, chan_list, src_list, live_list, dest_list, only=None):
     chan, dests = rel_ref.shape
     place = jnp.int32(0)
-    for b in range(dests):
+    for b in range(dests) if only is None else only:
         for k in range(chan):
             source = rel_ref[k, b]
             chan_list[place] = k
@@ -136,12 +131,12 @@
     return total
 
 
-def row_loop(blocks, rows, body, count):
+def row_loop(blocks, rows, body, count, first=0):
     zeros = tuple(jnp.zeros((CHUNK, LANES), F32) for _ in range(count))
     per = rows // CHUNK
 
     def step(n, carry):
-        return body(n // per, pl.ds(pl.multiple_of(lax.rem(n, per) * CHUNK, CHUNK), CHUNK), carry)
+        return body(first + n // per, pl.ds(pl.multiple_of(lax.rem(n, per) * CHUNK, CHUNK), CHUNK), carry)
 
     return lax.fori_loop(0, blocks * per, step, zeros)
 
@@ -155,30 +150,30 @@
     return jnp.where(den > 0, num / jnp.where(den > 0, den, 1.0), 0.0)
 
 
-def cut(b, x_ref, out_ref, sem):
-    copy = pltpu.make_async_copy(x_ref.at[pl.ds(b, 1)], out_ref, sem)
-    copy.start()
-    copy.wait()
+def cut(x_ref, *out_refs):
+    for b, out_ref in enumerate(out_refs):
+        out_ref[0] = x_ref[b]
 
 
 def first_local(
     rel_ref, ops_ref, x_ref, left_ref, right_ref,
     kron_ref, right_t_ref, image_ref, sums_ref,
-    mixed_ref, part_ref, chan_list, src_list, live_list, dest_list, fetched_ref, sem,
+    mixed_ref, part_ref, chan_list, src_list, live_list, dest_list, spread_ref, fetched_ref, sem,
 ):
     lists = (chan_list, src_list, live_list, dest_list)
     fetch = pltpu.make_async_copy(right_ref, fetched_ref, sem)
     fetch.start()
-    make_kron(ops_ref, kron_ref)
+    make_kron(ops_ref, kron_ref, spread_ref)
     chan, dests = left_ref.shape[:2]
     fetch.wait()
 
     def turn(n, carry):
-        k, b = n // dests, lax.rem(n, dests)
-        right_t_ref[k, b] = fetched_ref[k, b].T
+        for k in range(2):
+            for b in range(dests):
+                right_t_ref[2 * n + k, b] = fetched_ref[2 * n + k, b].T
         return carry
 
-    lax.fori_loop(0, chan * dests, turn, 0)
+    lax.fori_loop(0, chan // 2, turn, 0)
     image_ref[...] = jnp.zeros_like(image_ref)
     steps = list_pairs(rel_ref, 0, dests, *lists)
     add_pairs(steps, lists, kron_ref, x_ref, left_ref, right_t_ref, image_ref, mixed_ref, part_ref)
@@ -204,14 +199,18 @@
 
 
 def first_finish(
-    rel_ref, kron_ref, other_ref, left_ref, right_t_ref, before_ref, x_ref, image_ref, sums_ref,
-    acc_ref, guess_ref, out_sums_ref,
-    mixed_ref, part_ref, chan_list, src_list, live_list, dest_list,
-):
-    lists = (chan_list, src_list, live_list, dest_list)
+    dest, rel_ref, kron_ref, other_ref, left_ref, right_t_ref, before_ref, x_ref, image_ref,
+    sums_ref, *refs,
+):
     dests = left_ref.shape[1]
-    acc_ref[...] = before_ref[...]
-    steps = list_pairs(rel_ref, dests + 1, 2 * dests, *lists)
+    last = dest == dests - 1
+    if last:
+        earlier_ref, earlier_sums_ref, acc_ref, guess_ref, out_sums_ref, all_ref = refs[:6]
+    else:
+        acc_ref, guess_ref, out_sums_ref = refs[:3]
+    mixed_ref, part_ref = refs[-6:-4]
+    lists = refs[-4:]
+    steps = list_pairs(rel_ref, dests + 1, 2 * dests, *lists, only=(dest,))
     add_pairs(steps, lists, kron_ref, other_ref, left_ref, right_t_ref, acc_ref, mixed_ref, part_ref)
     num_local, den = sums_ref[0:1, :], sums_ref[1:2, :]
     shift = quotient(num_local, den)
@@ -220,11 +219,17 @@
     def sums(b, r, carry):
         x = x_ref[b, r, :].astype(F32)
         remote = acc_ref[b, r, :]
-        guess_ref[b, r, :] = (keep_state * x - STEP_SIZE * (image_ref[b, r, :] + remote)).astype(BF16)
+        guess = (keep_state * x - STEP_SIZE * (image_ref[b, r, :] + remote)).astype(BF16)
+        guess_ref[0, r, :] = guess
+        if last:
+            all_ref[b, r, :] = guess
         return (carry[0] + fold(x * remote),)
 
-    (num,) = row_loop(dests, x_ref.shape[1], sums, 1)
-    out_sums_ref[0:1, :] = num_local + jnp.sum(num)
+    (num,) = row_loop(1, x_ref.shape[1], sums, 1, first=dest)
+    out_sums_ref[0:1, :] = jnp.full((1, LANES), 1.0, F32) * jnp.sum(num)
+    if last:
+        out_sums_ref[0:1, :] += earlier_sums_ref[0:1, :] + num_local
+        all_ref[0:dest] = earlier_ref[...]
     out_sums_ref[1:2, :] = den
     out_sums_ref[2:3, :] = shift
     out_sums_ref[3:8, :] = jnp.zeros((5, LANES), F32)
@@ -249,7 +254,6 @@
 ):
     lists = (chan_list, src_list, live_list, dest_list)
     dests = left_ref.shape[1]
-    acc_ref[...] = before_ref[...]
     steps = list_pairs(rel_ref, dests, dests + 1, *lists)
     add_pairs(steps, lists, kron_ref, other_ref, left_ref, right_t_ref, acc_ref, mixed_ref, part_ref)
 
@@ -263,7 +267,6 @@
     lists = (chan_list, src_list, live_list, dest_list)
     dests, rows, width = x_ref.shape
     steps = list_pairs(rel_ref, dests + 1, 2 * dests, *lists)
-    kept_ref[...] = acc_ref[...]
     add_pairs(steps, lists, kron_ref, other_ref, left_ref, right_t_ref, kept_ref, mixed_ref, part_ref)
     energy = (mine_ref[0:1, :] + theirs_ref[0:1, :]) / (mine_ref[1:2, :] + theirs_ref[1:2, :])
     wide = functools.partial(jnp.tile, reps=(1, width // LANES))
@@ -305,25 +308,21 @@
     shift = STEP_SIZE * (both[0:1] / both[1:2] - mine_ref[5:6, :])
     norm = jnp.maximum(both[2:3] + shift * (2.0 * both[3:4] + shift * both[4:5]), 0.0)
     gain = jnp.sqrt(cells / (norm + EPSILON))
-    times = kept_ref.shape[2] // LANES
-    gain, shift = jnp.tile(gain, (1, times)), jnp.tile(shift, (1, times))
-
-    def one(b, r, carry):
-        state_ref[b, r, :] = (
-            (kept_ref[b, r, :] + shift * first_ref[b, r, :].astype(F32)) * gain
-        ).astype(BF16)
+    blocks, rows, width = kept_ref.shape
+    group = 4 * LANES
+    per = width // group
+
+    def one(n, carry):
+        b = n // per
+        for p in range(4):
+            cols = pl.ds(pl.multiple_of(lax.rem(n, per) * group + p * LANES, LANES), LANES)
+            kept = kept_ref[b, :, cols] + shift * first_ref[b, :, cols].astype(F32)
+            state = (kept * gain).astype(BF16)
+            state_ref[b, :, cols] = state
+            turned_ref[b, :, cols] = state.T
         return carry
 
-    blocks, rows, _ = kept_ref.shape
-    row_loop(blocks, rows, one, 0)
-
-    def turn(n, carry):
-        b, p = n // times, lax.rem(n, times)
-        cols = pl.ds(pl.multiple_of(p * LANES, LANES), LANES)
-        turned_ref[b, :, cols] = state_ref[b, :, cols].T
-        return carry
-
-    lax.fori_loop(0, blocks * times, turn, 0)
+    lax.fori_loop(0, blocks * per, one, 0)
 
 
 def environments(first, count, scale, env_ref, inner_ref, outer_ref, out_ref, mid_ref):
@@ -365,18 +364,15 @@
 def widen(places, *refs):
     pieces, outs, wides, sems = refs[:4], refs[4:6], refs[6:8], refs[8]
     copies = []
-    for n, (piece, (side, begin)) in enumerate(zip(pieces, places)):
-        count = piece.shape[0]
-
-        def one(k, carry):
-            wides[side][begin + k] = piece[k].astype(F32)
-            return carry
-
-        lax.fori_loop(0, count, one, 0)
-        span = pl.ds(begin, count)
-        copy = pltpu.make_async_copy(wides[side].at[span], outs[side].at[span], sems.at[n])
-        copy.start()
-        copies.append(copy)
+    for piece, (side, begin) in zip(pieces, places):
+        for n in range(0, piece.shape[0], 2):
+            span = pl.ds(begin + n, 2)
+            wides[side][begin + n : begin + n + 2] = piece[n : n + 2].astype(F32)
+            copy = pltpu.make_async_copy(
+                wides[side].at[span], outs[side].at[span], sems.at[len(copies)]
+            )
+            copy.start()
+            copies.append(copy)
     for copy in copies:
         copy.wait()
 
@@ -408,7 +404,7 @@
         pltpu.VMEM((2, rows, width), BF16), pltpu.VMEM((phys * rows, 2 * LANES), BF16)
     ] + lists
 
-    def call(body, specs, outs, scratch, *args):
+    def call(body, specs, outs, scratch, *args, aliases={}):
         return pl.pallas_call(
             body,
             in_specs=specs,
@@ -417,43 +413,53 @@
             scratch_shapes=scratch,
             compiler_params=PARAMS,
             cost_estimate=COST,
+            input_output_aliases=aliases,
         )(*args)
 
-    def block_of(b):
-        return call(
-            functools.partial(cut, b), [HBM], shape((1, rows, width), BF16),
-            [pltpu.SemaphoreType.DMA], x,
-        )
-
-    other = [trade(block_of(b)) for b in range(dests)]
+    block = shape((1, rows, width), BF16)
+    own = call(cut, [VMEM], (block,) * dests, [], x)
+    other = [trade(value) for value in own]
     kron, right_t, image_local, sums_local = call(
         first_local, [SMEM] + [VMEM] * 3 + [HBM],
         (shape((chan, phys * ROWS, phys * ROWS), BF16), shape(right.shape, BF16), wave_f32, sums_kind),
-        pair_scratch + [pltpu.VMEM(right.shape, BF16), pltpu.SemaphoreType.DMA],
+        pair_scratch
+        + [
+            pltpu.VMEM((chan * phys, phys * ROWS), F32),
+            pltpu.VMEM(right.shape, BF16),
+            pltpu.SemaphoreType.DMA,
+        ],
         rel, ops, x, left, right,
     )
     image_remote = call(
         first_remote, [SMEM] + [VMEM] * 4, wave_f32, pair_scratch,
         rel, kron, other[0], left, right_t,
     )
-    image_remote, guess, mine = call(
-        first_finish, [SMEM] + [VMEM] * 8, (wave_f32, wave_b16, sums_kind), pair_scratch,
+    image_remote, first_guess, some = call(
+        functools.partial(first_finish, 0), [SMEM] + [VMEM] * 8,
+        (wave_f32, block, sums_kind), pair_scratch,
         rel, kron, other[1], left, right_t, image_remote, x, image_local, sums_local,
-    )
+        aliases={5: 0},
+    )
+    image_remote, last_guess, mine, guess = call(
+        functools.partial(first_finish, 1), [SMEM] + [VMEM] * 10,
+        (wave_f32, block, sums_kind, wave_b16), pair_scratch,
+        rel, kron, other[1], left, right_t, image_remote, x, image_local, sums_local,
+        first_guess, some, aliases={5: 0},
+    )
+    other = [trade(first_guess), trade(last_guess)]
     theirs = trade(mine)
-    other = [trade(guess[b : b + 1]) for b in range(dests)]
     acc = call(
         second_local, [SMEM] + [VMEM] * 4, wave_f32, pair_scratch,
         rel, kron, guess, left, right_t,
     )
     acc = call(
         second_remote, [SMEM] + [VMEM] * 5, wave_f32, pair_scratch,
-        rel, kron, other[0], left, right_t, acc,
+        rel, kron, other[0], left, right_t, acc, aliases={5: 0},
     )
     kept, kept_first, sums_mine = call(
         second_finish, [SMEM, SMEM] + [VMEM] * 10, (wave_f32, wave_b16, sums_kind), pair_scratch,
         rel, ranks[0], kron, other[1], left, right_t, acc, x, image_local, image_remote,
-        mine, theirs,
+        mine, theirs, aliases={6: 0},
     )
     sums_theirs = trade(sums_mine)
 
@@ -497,7 +503,7 @@
         in_specs=[VMEM] * 4,
         out_specs=(HBM,) * 2,
         out_shape=(env_f32, env_f32),
-        scratch_shapes=[pltpu.VMEM(left.shape, F32)] * 2 + [pltpu.SemaphoreType.DMA((4,))],
+        scratch_shapes=[pltpu.VMEM(left.shape, F32)] * 2 + [pltpu.SemaphoreType.DMA((chan,))],
         compiler_params=PARAMS,
         cost_estimate=COST,
     )(lefts[0], rights[0], rights[1], lefts[1])

time: 109 us -> 102 us (0.936); the launches traced: 110 us -> 100 us
  Pallas kernels: 70.9 us -> 62.9 us
  waiting for transfers between devices: 17.2 us -> 10.3 us
  local copies, waits for them, and re-layouts: 1.52 us -> 5.82 us
    pallas_call x11, Pallas kernels: 61 us -> 55 us  [call(): pl.pallas_call(body, in_specs=specs, out_specs=jax.tree.map(lambda _: VME...]
    unnamed x14 -> x16, local copies, waits for them, and re-layouts: 1.32 us -> 5.72 us
    ppermute x6, waiting for transfers between devices: 7.58 us -> 4.01 us  [trade(): return lax.ppermute(value, 'blk', swap)]
    ppermute x4, waiting for transfers between devices: 9.64 us -> 6.27 us  [sent(): lax.ppermute(value, 'seg', [(s, s + steps) for s in range(begin, end)])]
    pallas_call x1, Pallas kernels: 7.91 us -> 5.96 us  [shards(): pl.pallas_call(functools.partial(normalize_and_left, 0, early, env_scale,...]
  transfers between devices with their start and end apart: 10 -> 10, of which waited for: 4 -> 3; matrix products, arithmetic and copies ran while one was open for 0% -> 1% of each run, Pallas kernels for 44% -> 45%
where the time goes in v3:
time: 102 us; the launch traced here: 100 us
  Pallas kernels  62.9 us (62%)
  starting transfers between devices  19.7 us (19%)
  waiting for transfers between devices  10.3 us (10%)
  local copies, waits for them, and re-layouts  5.82 us (6%)
    pallas_call x11, Pallas kernels, call(): pl.pallas_call(body, in_specs=specs, out_specs=jax.tree.map(lambda _: VME...  55 us
    ppermute x4, starting transfers between devices, sent(): lax.ppermute(value, 'seg', [(s, s + steps) for s in range(begin, end)])  11.3 us
    ppermute x6, starting transfers between devices, trade(): return lax.ppermute(value, 'blk', swap)  8.43 us
    ppermute x4, waiting for transfers between devices, sent(): lax.ppermute(value, 'seg', [(s, s + steps) for s in range(begin, end)])  6.27 us
    pallas_call x1, Pallas kernels, shards(): pl.pallas_call(functools.partial(normalize_and_left, 0, early, env_scale,...  5.96 us
    unnamed x16, local copies, waits for them, and re-layouts  5.72 us
    ppermute x6, waiting for transfers between devices, trade(): return lax.ppermute(value, 'blk', swap)  4.01 us
  transfers between devices with their start and end apart: 10, of which 3 were waited for; matrix products, arithmetic and copies ran while one was open for 1% of the time, Pallas kernels for 45%

profile of v3, /device:TPU:1, one launch (start us, length us, event | category | flops | bytes accessed | tf_op | source)
XLA Modules:
  0.0 100.4 jit_solution(7699799019454665537)
XLA Ops:
  0.6 0.0 copy-start.1
  0.6 0.0 copy-start.2
  0.7 1.3 %copy-done.2 = bf16[1,2,128,2048]{3,2,1,0:T(8,128)(2,1)S(1)} copy-done((bf16[1,2,128,2048]{3,2,1,0:T(8,128)(2,1)S(1)}, bf16[1,2,128,2048]{3,2,1,0:T(8,128)(2,1)}, u32[]{:S(2)}) %copy-start.2) | copy-done | bytes 1048600
  1.9 0.1 shard_map.86
  2.0 2.1 %collective-permute-start.1 = (bf16[1,128,2048]{2,1,0:T(8,128)(2,1)S(1)}, bf16[1,128,2048]{2,1,0:T(8,128)(2,1)S(1)}, u32[]{:S(2)}, u32[]{:S(2)}) collective-permute-start(bf16[1,128,2048]{2,1,0:T(8,128)(2,1)S(1)} %get-tuple-element.28), channel_id=1, source_target_pairs={{0,1},{1,0},{2,3},{3,2},{4,5},{5,4},{6,7},{7,6},{8,9},{9,8},{10,11... | collective-permute-start | bytes 1572872 | tf_op jit(solution)/shard_map/ppermute | solution.py:393
  4.1 0.1 collective-permute-start
  4.2 0.7 add_bitcast_fusion
  4.9 0.1 copy.13
  5.0 0.0 copy-start
  5.0 1.2 %copy-done = bf16[1,14,2,128,128]{4,3,2,1,0:T(8,128)(2,1)S(1)} copy-done((bf16[1,14,2,128,128]{4,3,2,1,0:T(8,128)(2,1)S(1)}, bf16[1,14,2,128,128]{4,3,2,1,0:T(8,128)(2,1)}, u32[]{:S(2)}) %copy-start) | copy-done | bytes 917528
  6.2 0.0 copy-start.3
  6.2 1.2 %copy-done.3 = bf16[1,2,128,2048]{3,2,1,0:T(8,128)(2,1)S(1)} copy-done((bf16[1,2,128,2048]{3,2,1,0:T(8,128)(2,1)S(1)}, bf16[1,2,128,2048]{3,2,1,0:T(8,128)(2,1)}, u32[]{:S(2)}) %copy-start.3) | copy-done | bytes 1048600
  7.4 0.0 copy-start.4
  7.4 1.2 %copy-done.4 = bf16[1,14,2,128,128]{4,3,2,1,0:T(8,128)(2,1)S(1)} copy-done((bf16[1,14,2,128,128]{4,3,2,1,0:T(8,128)(2,1)S(1)}, bf16[1,14,2,128,128]{4,3,2,1,0:T(8,128)(2,1)}, u32[]{:S(2)}) %copy-start.4) | copy-done | bytes 917528
  8.6 0.0 copy-start.6
  8.6 0.8 copy-done.6
  9.4 12.2 %shard_map.85 = (bf16[14,256,256]{2,1,0:T(8,128)(2,1)S(1)}, bf16[14,2,128,128]{3,2,1,0:T(8,128)(2,1)S(1)}, f32[2,128,2048]{2,1,0:T(8,128)S(1)}, f32[8,128]{1,0:T(8,128)S(1)}) custom-call(s32[14,2]{1,0:T(8,128)S(1)} %negate_select_fusion.rel_ref, bf16[14,16,16]{2,1,0:T(8,128)(2,1)S(1)} %bitcast.27, bf16[2,128,2048]{2,1,0:T(8,128)(2,1)S(1)} %bitcast.20, ...), custom_call_target="tpu_custom_call" | custom-call | flops 1024 | bytes 1024 | tf_op jit(solution)/shard_map/pallas_call | solution.py:408
  21.6 0.0 collective-permute-done.1.other_ref
  21.6 0.0 copy-done.1
  21.6 5.4 %shard_map.87.before_ref = f32[2,128,2048]{2,1,0:T(8,128)S(1)} custom-call(s32[14,2]{1,0:T(8,128)S(1)} %negate_select_fusion.rel_ref, bf16[14,256,256]{2,1,0:T(8,128)(2,1)S(1)} %get-tuple-element.25.kron_ref, bf16[1,128,2048]{2,1,0:T(8,128)(2,1)S(1)} %collective-permute-done.1.other_ref, bf16[14,2,128,128]{3,2,1,0:T(8,128)(2,1)S(1)} %bitcast.11, ...), custom_call_target="tpu_custom_call" | custom-call | flops 1024 | bytes 1024 | tf_op jit(solution)/shard_map/pallas_call | solution.py:408
  27.0 0.0 collective-permute-done.other_ref
  27.0 3.6 %shard_map.88 = (f32[2,128,2048]{2,1,0:T(8,128)S(1)}, bf16[1,128,2048]{2,1,0:T(8,128)(2,1)S(1)}, f32[8,128]{1,0:T(8,128)S(1)}) custom-call(s32[14,2]{1,0:T(8,128)S(1)} %negate_select_fusion.rel_ref, bf16[14,256,256]{2,1,0:T(8,128)(2,1)S(1)} %get-tuple-element.25.kron_ref, ...), custom_call_target="tpu_custom_call", output_to_operand_aliasing={{0}: (5, {})} | custom-call | flops 1024 | bytes 1024 | tf_op jit(solution)/shard_map/pallas_call | solution.py:408
  30.7 2.2 %collective-permute-start.3 = (bf16[1,128,2048]{2,1,0:T(8,128)(2,1)S(1)}, bf16[1,128,2048]{2,1,0:T(8,128)(2,1)S(1)}, u32[]{:S(2)}, u32[]{:S(2)}) collective-permute-start(bf16[1,128,2048]{2,1,0:T(8,128)(2,1)S(1)} %get-tuple-element.32.refs_0_), channel_id=1, source_target_pairs={{0,1},{1,0},{2,3},{3,2},{4,5},{5,4},{6,7},{7,6},{8,9},{9,8},{10,11... | collective-permute-start | bytes 1572872 | tf_op jit(solution)/shard_map/ppermute | solution.py:393
  32.9 2.6 %shard_map.89 = (f32[2,128,2048]{2,1,0:T(8,128)S(1)}, bf16[1,128,2048]{2,1,0:T(8,128)(2,1)S(1)}, f32[8,128]{1,0:T(8,128)S(1)}, bf16[2,128,2048]{2,1,0:T(8,128)(2,1)S(1)}) custom-call(s32[14,2]{1,0:T(8,128)S(1)} %negate_select_fusion.rel_ref, bf16[14,256,256]{2,1,0:T(8,128)(2,1)S(1)} %get-tuple-element.25.kron_ref, ...), custom_call_target="tpu_custom_call", output_to_operand_aliasing={{0}: (5, {})} | custom-call | flops 1024 | bytes 1024 | tf_op jit(solution)/shard_map/pallas_call | solution.py:408
  35.5 0.1 collective-permute-start.2
  35.6 1.4 %collective-permute-start.4 = (f32[8,128]{1,0:T(8,128)S(1)}, f32[8,128]{1,0:T(8,128)S(1)}, u32[]{:S(2)}, u32[]{:S(2)}) collective-permute-start(f32[8,128]{1,0:T(8,128)S(1)} %get-tuple-element.37.mine_ref), channel_id=1, source_target_pairs={{0,1},{1,0},{2,3},{3,2},{4,5},{5,4},{6,7},{7,6},{8,9},{9,8},{10,11... | collective-permute-start | bytes 12296 | tf_op jit(solution)/shard_map/ppermute | solution.py:393
  37.0 10.4 %shard_map.90.before_ref = f32[2,128,2048]{2,1,0:T(8,128)S(1)} custom-call(s32[14,2]{1,0:T(8,128)S(1)} %negate_select_fusion.rel_ref, bf16[14,256,256]{2,1,0:T(8,128)(2,1)S(1)} %get-tuple-element.25.kron_ref, bf16[2,128,2048]{2,1,0:T(8,128)(2,1)S(1)} %get-tuple-element.35.guess_ref, bf16[14,2,128,128]{3,2,1,0:T(8,128)(2,1)S(1)} %bitcast.14, ...), custom_call_target="tpu_custom_call" | custom-call | flops 1024 | bytes 1024 | tf_op jit(solution)/shard_map/pallas_call | solution.py:408
  47.4 0.0 copy-start.7
  47.4 0.0 collective-permute-done.3.other_ref
  47.4 5.3 %shard_map.91.acc_ref = f32[2,128,2048]{2,1,0:T(8,128)S(1)} custom-call(s32[14,2]{1,0:T(8,128)S(1)} %negate_select_fusion.rel_ref, bf16[14,256,256]{2,1,0:T(8,128)(2,1)S(1)} %get-tuple-element.25.kron_ref, bf16[1,128,2048]{2,1,0:T(8,128)(2,1)S(1)} %collective-permute-done.3.other_ref, ...), custom_call_target="tpu_custom_call", output_to_operand_aliasing={{}: (5, {})} | custom-call | flops 1024 | bytes 1024 | tf_op jit(solution)/shard_map/pallas_call | solution.py:408
  52.7 3.0 %collective-permute-done.4.theirs_ref = f32[8,128]{1,0:T(8,128)S(1)} collective-permute-done((f32[8,128]{1,0:T(8,128)S(1)}, f32[8,128]{1,0:T(8,128)S(1)}, u32[]{:S(2)}, u32[]{:S(2)}) %collective-permute-start.4) | collective-permute-done | bytes 4128 | tf_op jit(solution)/shard_map/ppermute | solution.py:393
  55.7 0.0 collective-permute-done.2.other_ref
  55.7 0.0 copy-done.7
  55.7 6.4 %shard_map.92 = (f32[2,128,2048]{2,1,0:T(8,128)S(1)}, bf16[2,128,2048]{2,1,0:T(8,128)(2,1)S(1)}, f32[8,128]{1,0:T(8,128)S(1)}) custom-call(s32[14,2]{1,0:T(8,128)S(1)} %negate_select_fusion.rel_ref, s32[2]{0:T(128)S(1)} %bitcast.28, bf16[14,256,256]{2,1,0:T(8,128)(2,1)S(1)} %get-tuple-element.25.kron_ref, ...), custom_call_target="tpu_custom_call", output_to_operand_aliasing={{0}: (6, {})} | custom-call | flops 1024 | bytes 1024 | tf_op jit(solution)/shard_map/pallas_call | solution.py:408
  62.1 0.0 copy-start.5
  62.1 2.5 %collective-permute-start.5 = (f32[8,128]{1,0:T(8,128)S(1)}, f32[8,128]{1,0:T(8,128)S(1)}, u32[]{:S(2)}, u32[]{:S(2)}) collective-permute-start(f32[8,128]{1,0:T(8,128)S(1)} %get-tuple-element.40.mine_ref), channel_id=1, source_target_pairs={{0,1},{1,0},{2,3},{3,2},{4,5},{5,4},{6,7},{7,6},{8,9},{9,8},{10,11... | collective-permute-start | bytes 12296 | tf_op jit(solution)/shard_map/ppermute | solution.py:393
  64.7 1.0 collective-permute-done.5.theirs_ref
  65.7 6.0 %shard_map.93 = (bf16[2,128,2048]{2,1,0:T(8,128)(2,1)}, bf16[2,128,2048]{2,1,0:T(8,128)(2,1)S(1)}, bf16[2,128,2048]{2,1,0:T(8,128)(2,1)S(1)}, bf16[10,2,128,128]{3,2,1,0:T(8,128)(2,1)S(1)}) custom-call(f32[2,128,2048]{2,1,0:T(8,128)S(1)} %get-tuple-element.38.kept_ref, bf16[2,128,2048]{2,1,0:T(8,128)(2,1)S(1)} %get-tuple-element.39.first_ref, ...), custom_call_target="tpu_custom_call" | custom-call | flops 1024 | bytes 1024 | tf_op jit(solution)/shard_map/pallas_call | solution.py:485
  71.6 3.8 %collective-permute-start.6 = (bf16[10,2,128,128]{3,2,1,0:T(8,128)(2,1)S(1)}, bf16[10,2,128,128]{3,2,1,0:T(8,128)(2,1)S(1)}, u32[]{:S(2)}, u32[]{:S(2)}) collective-permute-start(bf16[10,2,128,128]{3,2,1,0:T(8,128)(2,1)S(1)} %get-tuple-element.42), channel_id=1, source_target_pairs={{0,2},{2,4},{4,6},{6,8},{8,10},{10,12},{12,14},{14,16},{16,18},{18... | collective-permute-start | bytes 1966088 | tf_op jit(solution)/shard_map/ppermute | solution.py:474
  75.4 0.0 copy-done.5
  75.4 4.1 %shard_map.94 = bf16[8,2,128,128]{3,2,1,0:T(8,128)(2,1)S(1)} custom-call(bf16[14,2,128,128]{3,2,1,0:T(8,128)(2,1)S(1)} %bitcast.25, bf16[2,128,2048]{2,1,0:T(8,128)(2,1)S(1)} %get-tuple-element.43.inner_ref.outer_ref, bf16[2,128,2048]{2,1,0:T(8,128)(2,1)S(1)} %get-tuple-element.44.outer_ref.inner_ref), custom_call_target="tpu_custom_call" | custom-call | flops 1024 | bytes 1024 | tf_op jit(solution)/shard_map/pallas_call | solution.py:408
  79.5 1.9 %collective-permute-start.7 = (bf16[8,2,128,128]{3,2,1,0:T(8,128)(2,1)S(1)}, bf16[8,2,128,128]{3,2,1,0:T(8,128)(2,1)S(1)}, u32[]{:S(2)}, u32[]{:S(2)}) collective-permute-start(bf16[8,2,128,128]{3,2,1,0:T(8,128)(2,1)S(1)} %shard_map.94), channel_id=1, source_target_pairs={{2,0},{4,2},{6,4},{8,6},{10,8},{12,10},{14,12},{16,14},{18,16},{20... | collective-permute-start | bytes 1572872 | tf_op jit(solution)/shard_map/ppermute | solution.py:474
  81.4 3.0 %shard_map.95 = bf16[6,2,128,128]{3,2,1,0:T(8,128)(2,1)S(1)} custom-call(bf16[14,2,128,128]{3,2,1,0:T(8,128)(2,1)S(1)} %bitcast.26, bf16[2,128,2048]{2,1,0:T(8,128)(2,1)S(1)} %get-tuple-element.43.inner_ref.outer_ref, bf16[2,128,2048]{2,1,0:T(8,128)(2,1)S(1)} %get-tuple-element.44.outer_ref.inner_ref), custom_call_target="tpu_custom_call" | custom-call | flops 1024 | bytes 1024 | tf_op jit(solution)/shard_map/pallas_call | solution.py:408
  84.5 1.9 %collective-permute-start.8 = (bf16[6,2,128,128]{3,2,1,0:T(8,128)(2,1)S(1)}, bf16[6,2,128,128]{3,2,1,0:T(8,128)(2,1)S(1)}, u32[]{:S(2)}, u32[]{:S(2)}) collective-permute-start(bf16[6,2,128,128]{3,2,1,0:T(8,128)(2,1)S(1)} %shard_map.95), channel_id=1, source_target_pairs={{2,0},{4,2},{6,4},{8,6},{10,8},{12,10},{14,12},{16,14},{18,16},{20... | collective-permute-start | bytes 1179656 | tf_op jit(solution)/shard_map/ppermute | solution.py:474
  86.4 1.9 %shard_map.96 = bf16[4,2,128,128]{3,2,1,0:T(8,128)(2,1)S(1)} custom-call(bf16[14,2,128,128]{3,2,1,0:T(8,128)(2,1)S(1)} %bitcast.18, bf16[2,128,2048]{2,1,0:T(8,128)(2,1)S(1)} %get-tuple-element.44.outer_ref.inner_ref, bf16[2,128,2048]{2,1,0:T(8,128)(2,1)S(1)} %get-tuple-element.43.inner_ref.outer_ref), custom_call_target="tpu_custom_call" | custom-call | flops 1024 | bytes 1024 | tf_op jit(solution)/shard_map/pallas_call | solution.py:408
  88.4 3.6 %collective-permute-start.9 = (bf16[4,2,128,128]{3,2,1,0:T(8,128)(2,1)S(1)}, bf16[4,2,128,128]{3,2,1,0:T(8,128)(2,1)S(1)}, u32[]{:S(2)}, u32[]{:S(2)}) collective-permute-start(bf16[4,2,128,128]{3,2,1,0:T(8,128)(2,1)S(1)} %shard_map.96), channel_id=1, source_target_pairs={{0,2},{2,4},{4,6},{6,8},{8,10},{10,12},{12,14},{14,16},{16,18},{18... | collective-permute-start | bytes 786440 | tf_op jit(solution)/shard_map/ppermute | solution.py:474
  92.0 6.3 %collective-permute-done.9.refs_3_ = bf16[4,2,128,128]{3,2,1,0:T(8,128)(2,1)S(1)} collective-permute-done((bf16[4,2,128,128]{3,2,1,0:T(8,128)(2,1)S(1)}, bf16[4,2,128,128]{3,2,1,0:T(8,128)(2,1)S(1)}, u32[]{:S(2)}, u32[]{:S(2)}) %collective-permute-start.9) | collective-permute-done | bytes 262176 | tf_op jit(solution)/shard_map/ppermute | solution.py:474
  98.3 0.0 collective-permute-done.8.refs_2_
  98.3 0.0 collective-permute-done.7.refs_1_
  98.3 0.0 collective-permute-done.6.refs_0_
  98.3 2.0 %shard_map.97 = (f32[14,2,128,128]{3,2,1,0:T(8,128)}, f32[14,2,128,128]{3,2,1,0:T(8,128)}) custom-call(bf16[10,2,128,128]{3,2,1,0:T(8,128)(2,1)S(1)} %collective-permute-done.6.refs_0_, bf16[8,2,128,128]{3,2,1,0:T(8,128)(2,1)S(1)} %collective-permute-done.7.refs_1_, bf16[6,2,128,128]{3,2,1,0:T(8,128)(2,1)S(1)} %collective-permute-done.8.refs_2_, ...), custom_call_target="tpu_custom_call" | custom-call | flops 1024 | bytes 1024 | tf_op jit(solution)/shard_map/pallas_call | solution.py:501
  (1 shorter events, 0.0 us)
Async XLA Ops:
  0.6 21.0 %copy-start.1 = (bf16[1,14,2,128,128]{4,3,2,1,0:T(8,128)(2,1)S(1)}, bf16[1,14,2,128,128]{4,3,2,1,0:T(8,128)(2,1)}, u32[]{:S(2)}) copy-start(bf16[1,14,2,128,128]{4,3,2,1,0:T(8,128)(2,1)} %param.7) | copy-start | bytes 2752516
  0.6 1.3 %copy-start.2 = (bf16[1,2,128,2048]{3,2,1,0:T(8,128)(2,1)S(1)}, bf16[1,2,128,2048]{3,2,1,0:T(8,128)(2,1)}, u32[]{:S(2)}) copy-start(bf16[1,2,128,2048]{3,2,1,0:T(8,128)(2,1)} %param.6) | copy-start | bytes 3145732
  2.0 19.6 %collective-permute-start.1 = (bf16[1,128,2048]{2,1,0:T(8,128)(2,1)S(1)}, bf16[1,128,2048]{2,1,0:T(8,128)(2,1)S(1)}, u32[]{:S(2)}, u32[]{:S(2)}) collective-permute-start(bf16[1,128,2048]{2,1,0:T(8,128)(2,1)S(1)} %get-tuple-element.28), channel_id=1, source_target_pairs={{0,1},{1,0},{2,3},{3,2},{4,5},{5,4},{6,7},{7,6},{8,9},{9,8},{10,11... | collective-permute-start | bytes 1572872 | tf_op jit(solution)/shard_map/ppermute | solution.py:393
  4.1 22.9 %collective-permute-start = (bf16[1,128,2048]{2,1,0:T(8,128)(2,1)S(1)}, bf16[1,128,2048]{2,1,0:T(8,128)(2,1)S(1)}, u32[]{:S(2)}, u32[]{:S(2)}) collective-permute-start(bf16[1,128,2048]{2,1,0:T(8,128)(2,1)S(1)} %get-tuple-element.26), channel_id=1, source_target_pairs={{0,1},{1,0},{2,3},{3,2},{4,5},{5,4},{6,7},{7,6},{8,9},{9,8},{10,11... | collective-permute-start | bytes 1572872 | tf_op jit(solution)/shard_map/ppermute | solution.py:393
  5.0 1.2 %copy-start = (bf16[1,14,2,128,128]{4,3,2,1,0:T(8,128)(2,1)S(1)}, bf16[1,14,2,128,128]{4,3,2,1,0:T(8,128)(2,1)}, u32[]{:S(2)}) copy-start(bf16[1,14,2,128,128]{4,3,2,1,0:T(8,128)(2,1)} %param.7) | copy-start | bytes 2752516
  6.2 1.2 %copy-start.3 = (bf16[1,2,128,2048]{3,2,1,0:T(8,128)(2,1)S(1)}, bf16[1,2,128,2048]{3,2,1,0:T(8,128)(2,1)}, u32[]{:S(2)}) copy-start(bf16[1,2,128,2048]{3,2,1,0:T(8,128)(2,1)} %param.6) | copy-start | bytes 3145732
  7.4 1.2 %copy-start.4 = (bf16[1,14,2,128,128]{4,3,2,1,0:T(8,128)(2,1)S(1)}, bf16[1,14,2,128,128]{4,3,2,1,0:T(8,128)(2,1)}, u32[]{:S(2)}) copy-start(bf16[1,14,2,128,128]{4,3,2,1,0:T(8,128)(2,1)} %param.8) | copy-start | bytes 2752516
  8.6 0.8 copy-start.6
  30.7 16.7 %collective-permute-start.3 = (bf16[1,128,2048]{2,1,0:T(8,128)(2,1)S(1)}, bf16[1,128,2048]{2,1,0:T(8,128)(2,1)S(1)}, u32[]{:S(2)}, u32[]{:S(2)}) collective-permute-start(bf16[1,128,2048]{2,1,0:T(8,128)(2,1)S(1)} %get-tuple-element.32.refs_0_), channel_id=1, source_target_pairs={{0,1},{1,0},{2,3},{3,2},{4,5},{5,4},{6,7},{7,6},{8,9},{9,8},{10,11... | collective-permute-start | bytes 1572872 | tf_op jit(solution)/shard_map/ppermute | solution.py:393
  35.5 20.2 %collective-permute-start.2 = (bf16[1,128,2048]{2,1,0:T(8,128)(2,1)S(1)}, bf16[1,128,2048]{2,1,0:T(8,128)(2,1)S(1)}, u32[]{:S(2)}, u32[]{:S(2)}) collective-permute-start(bf16[1,128,2048]{2,1,0:T(8,128)(2,1)S(1)} %get-tuple-element.34), channel_id=1, source_target_pairs={{0,1},{1,0},{2,3},{3,2},{4,5},{5,4},{6,7},{7,6},{8,9},{9,8},{10,11... | collective-permute-start | bytes 1572872 | tf_op jit(solution)/shard_map/ppermute | solution.py:393
  35.6 20.1 %collective-permute-start.4 = (f32[8,128]{1,0:T(8,128)S(1)}, f32[8,128]{1,0:T(8,128)S(1)}, u32[]{:S(2)}, u32[]{:S(2)}) collective-permute-start(f32[8,128]{1,0:T(8,128)S(1)} %get-tuple-element.37.mine_ref), channel_id=1, source_target_pairs={{0,1},{1,0},{2,3},{3,2},{4,5},{5,4},{6,7},{7,6},{8,9},{9,8},{10,11... | collective-permute-start | bytes 12296 | tf_op jit(solution)/shard_map/ppermute | solution.py:393
  47.4 8.3 %copy-start.7 = (s32[1,2]{1,0:T(1,128)S(1)}, s32[1,2]{1,0:T(1,128)}, u32[]{:S(2)}) copy-start(s32[1,2]{1,0:T(1,128)} %param.11) | copy-start | bytes 28
  62.1 13.3 %copy-start.5 = (bf16[1,14,2,128,128]{4,3,2,1,0:T(8,128)(2,1)S(1)}, bf16[1,14,2,128,128]{4,3,2,1,0:T(8,128)(2,1)}, u32[]{:S(2)}) copy-start(bf16[1,14,2,128,128]{4,3,2,1,0:T(8,128)(2,1)} %param.8) | copy-start | bytes 2752516
  62.1 3.5 %collective-permute-start.5 = (f32[8,128]{1,0:T(8,128)S(1)}, f32[8,128]{1,0:T(8,128)S(1)}, u32[]{:S(2)}, u32[]{:S(2)}) collective-permute-start(f32[8,128]{1,0:T(8,128)S(1)} %get-tuple-element.40.mine_ref), channel_id=1, source_target_pairs={{0,1},{1,0},{2,3},{3,2},{4,5},{5,4},{6,7},{7,6},{8,9},{9,8},{10,11... | collective-permute-start | bytes 12296 | tf_op jit(solution)/shard_map/ppermute | solution.py:393
  71.6 26.7 %collective-permute-start.6 = (bf16[10,2,128,128]{3,2,1,0:T(8,128)(2,1)S(1)}, bf16[10,2,128,128]{3,2,1,0:T(8,128)(2,1)S(1)}, u32[]{:S(2)}, u32[]{:S(2)}) collective-permute-start(bf16[10,2,128,128]{3,2,1,0:T(8,128)(2,1)S(1)} %get-tuple-element.42), channel_id=1, source_target_pairs={{0,2},{2,4},{4,6},{6,8},{8,10},{10,12},{12,14},{14,16},{16,18},{18... | collective-permute-start | bytes 1966088 | tf_op jit(solution)/shard_map/ppermute | solution.py:474
  79.5 18.8 %collective-permute-start.7 = (bf16[8,2,128,128]{3,2,1,0:T(8,128)(2,1)S(1)}, bf16[8,2,128,128]{3,2,1,0:T(8,128)(2,1)S(1)}, u32[]{:S(2)}, u32[]{:S(2)}) collective-permute-start(bf16[8,2,128,128]{3,2,1,0:T(8,128)(2,1)S(1)} %shard_map.94), channel_id=1, source_target_pairs={{2,0},{4,2},{6,4},{8,6},{10,8},{12,10},{14,12},{16,14},{18,16},{20... | collective-permute-start | bytes 1572872 | tf_op jit(solution)/shard_map/ppermute | solution.py:474
  84.5 13.8 %collective-permute-start.8 = (bf16[6,2,128,128]{3,2,1,0:T(8,128)(2,1)S(1)}, bf16[6,2,128,128]{3,2,1,0:T(8,128)(2,1)S(1)}, u32[]{:S(2)}, u32[]{:S(2)}) collective-permute-start(bf16[6,2,128,128]{3,2,1,0:T(8,128)(2,1)S(1)} %shard_map.95), channel_id=1, source_target_pairs={{2,0},{4,2},{6,4},{8,6},{10,8},{12,10},{14,12},{16,14},{18,16},{20... | collective-permute-start | bytes 1179656 | tf_op jit(solution)/shard_map/ppermute | solution.py:474
  88.4 9.9 %collective-permute-start.9 = (bf16[4,2,128,128]{3,2,1,0:T(8,128)(2,1)S(1)}, bf16[4,2,128,128]{3,2,1,0:T(8,128)(2,1)S(1)}, u32[]{:S(2)}, u32[]{:S(2)}) collective-permute-start(bf16[4,2,128,128]{3,2,1,0:T(8,128)(2,1)S(1)} %shard_map.96), channel_id=1, source_target_pairs={{0,2},{2,4},{4,6},{6,8},{8,10},{10,12},{12,14},{14,16},{16,18},{18... | collective-permute-start | bytes 786440 | tf_op jit(solution)/shard_map/ppermute | solution.py:474
